TPU v7x, 32 devices: a whole 2x2x4 slice. The times are simulated.
32 devices in a mesh: groups: 2 (over y), points: 4 (over z), centers: 4 (over x, core).
Axes of the slice: x: 2, y: 2, z: 4, core: 2. Of those that a mesh axis runs over, the one named last changes fastest.
Arguments:
- train_points: bfloat16 [8192, 512], P(('groups', 'points')), parts along dimension 0, may hold values from -6 to 6
- saved_preds: float32 [8192, 128], P(('groups', 'points')), parts along dimension 0, may hold values from -6 to 6
- targets: float32 [8192, 128], P(('groups', 'points')), parts along dimension 0, may hold values from -6 to 6
- huber_delta: float32 [256], P('groups'), parts along dimension 0, may hold values from 0.3 to 3
- center_pos: bfloat16 [16384, 512], P(('groups', 'points', 'centers')), parts along dimension 0, may hold values from -6 to 6
- coefficients: bfloat16 [16384, 128], P(('groups', 'points', 'centers')), parts along dimension 0, may hold values from -0.8984375 to 0.8984375
- spread: bfloat16 [16384], P(('groups', 'points', 'centers')), parts along dimension 0, may hold values from 0.5 to 2
Outputs:
- grad_centers: float32 [16384, 512], P(('groups', 'points', 'centers')), parts along dimension 0
- grad_coef: float32 [16384, 128], P(('groups', 'points', 'centers')), parts along dimension 0
There are 2 independent parts, one for each index of `groups`. A program takes and returns all parts, laid end to end along the dimension named above; each array names one. Nothing has to cross between parts.
All inputs are finite; a program needn't handle non-finite values.
Results may differ from a plain program's by a relative error of at most 0.0003.
Values may be sent and summed in bfloat16 or wider, within the bound.
A program may use at most 64 MiB of HBM per device.

v0:
```python
import jax
import jax.numpy as jnp
from jax import lax
from jax.sharding import PartitionSpec as P


def per_device(train_points, saved_preds, targets, huber_delta, center_pos, coefficients, spread):
    n_points, in_width = train_points.shape
    whole_pos, whole_coef, whole_rates = (
        lax.all_gather(center_pos, "points", axis=0, tiled=True),
        lax.all_gather(coefficients, "points", axis=0, tiled=True),
        lax.all_gather(spread, "points", axis=0, tiled=True),
    )
    center_sq = jnp.sum(jnp.square(whole_pos.astype(jnp.float32)), axis=1)
    rates = whole_rates.astype(jnp.float32)
    panel_width = whole_pos.shape[0]
    out_width = whole_coef.shape[1]
    block_rows = min(512, n_points)
    block_count = n_points // block_rows
    point_blocks = train_points.reshape(block_count, block_rows, in_width)

    def kernel_of(row_block):
        point_sq = jnp.sum(jnp.square(row_block.astype(jnp.float32)), axis=1)
        cross = lax.dot_general(
            row_block, whole_pos, (((1,), (1,)), ((), ())), preferred_element_type=jnp.float32
        )
        dist = point_sq[:, None] + center_sq[None, :] - 2.0 * cross
        return jnp.exp(-rates[None, :] * dist / in_width).astype(jnp.bfloat16)

    kernels = lax.map(kernel_of, point_blocks)
    partial_pred = jnp.dot(
        kernels.reshape(n_points, panel_width), whole_coef, preferred_element_type=jnp.float32
    )
    panel_pred = lax.psum(partial_pred, "centers")
    residual = panel_pred + saved_preds - targets
    cotangent = (residual / jnp.sqrt(1.0 + jnp.square(residual / huber_delta[None, :]))).astype(
        jnp.bfloat16
    )
    cot_blocks = cotangent.reshape(block_count, block_rows, out_width)

    def coef_term(kernel, cot_block):
        return lax.dot_general(
            kernel, cot_block, (((0,), (0,)), ((), ())), preferred_element_type=jnp.float32
        )

    def moment_terms(kernel, cot_block, row_block):
        mixing = lax.dot_general(
            cot_block, whole_coef, (((1,), (1,)), ((), ())), preferred_element_type=jnp.float32
        )
        weights = (kernel.astype(jnp.float32) * mixing).astype(jnp.bfloat16)
        totals = jnp.sum(weights.astype(jnp.float32), axis=0)
        moment = lax.dot_general(
            weights, row_block, (((0,), (0,)), ((), ())), preferred_element_type=jnp.float32
        )
        return (moment, totals)

    zero_coef = jnp.zeros((panel_width, out_width), jnp.float32)
    zero_moment = jnp.zeros((panel_width, in_width), jnp.float32)
    zero_totals = jnp.zeros((panel_width,), jnp.float32)

    def coef_pass(coef_acc, inputs):
        row_block, stored, cot_block = inputs
        return (coef_acc + coef_term(stored, cot_block), None)

    coef_acc, _ = lax.scan(coef_pass, zero_coef, (point_blocks, kernels, cot_blocks))
    grad_coef = lax.psum_scatter(coef_acc, "points", scatter_dimension=0, tiled=True)

    def moment_pass(totals, inputs):
        moment_acc, totals_acc = totals
        row_block, stored, cot_block = inputs
        moment, row_sum = moment_terms(stored, cot_block, row_block)
        return ((moment_acc + moment, totals_acc + row_sum), None)

    (moment_acc, totals_acc), _ = lax.scan(
        moment_pass, (zero_moment, zero_totals), (point_blocks, kernels, cot_blocks)
    )
    own_moment, own_totals = (
        lax.psum_scatter(moment_acc, "points", scatter_dimension=0, tiled=True),
        lax.psum_scatter(totals_acc, "points", scatter_dimension=0, tiled=True),
    )
    own_rates = spread.astype(jnp.float32)
    grad_centers = (2.0 * own_rates / in_width)[:, None] * (
        own_moment - own_totals[:, None] * center_pos.astype(jnp.float32)
    )
    return (grad_centers, grad_coef)


def solution(mesh):
    return jax.shard_map(
        per_device,
        mesh=mesh,
        in_specs=(
            P(("groups", "points"), None),
            P(("groups", "points"), None),
            P(("groups", "points"), None),
            P("groups"),
            P(("groups", "points", "centers"), None),
            P(("groups", "points", "centers"), None),
            P(("groups", "points", "centers")),
        ),
        out_specs=(
            P(("groups", "points", "centers"), None),
            P(("groups", "points", "centers"), None),
        ),
        check_vma=False,
    )
```

profile of v0, /device:TPU:0, one launch (start us, length us, event | category | flops | bytes accessed | tf_op | source)
XLA Modules:
  0.0 246.5 jit_solution(6114186068954046954)
XLA Ops:
  7.2 0.0 all-gather.3.cloned.1.call-start
  7.2 0.7 all-gather.3.cloned.1.call-update
  7.9 0.0 all-reduce.3.cloned.1.call-start
  8.0 0.7 reshape.29
  8.6 13.5 %all-gather = bf16[4,1,512]{2,1,0:T(2,128)(2,1)S(1)} all-gather(bf16[1,1,512]{2,1,0:T(2,128)(2,1)S(1)} %reshape.29), channel_id=1, replica_groups=mesh['groups'=2,'points'=4,'centers'=4] {'points'}, dimensions={0}, use_global_device_ids=true | all-gather | bytes 5120 | tf_op jit(solution)/shard_map/all_gather | solution.py:12
  22.2 22.0 %all_gather.11 = bf16[2048,128]{1,0:T(8,128)(2,1)} all-gather(bf16[512,128]{1,0:T(8,128)(2,1)} %param.18), channel_id=1, replica_groups=mesh['groups'=2,'points'=4,'centers'=4] {'points'}, dimensions={0}, use_global_device_ids=true | all-gather | bytes 655360 | tf_op jit(solution)/shard_map/all_gather | solution.py:11
  44.2 22.4 %all-gather.3.cloned.1.call-done = bf16[2048,512]{1,0:T(8,128)(2,1)} async-done(((bf16[512,512]{1,0:T(8,128)(2,1)}), bf16[2048,512]{1,0:T(8,128)(2,1)}) %all-gather.3.cloned.1.call-update) | async-done | bytes 2097168 | tf_op jit(solution)/shard_map/all_gather | solution.py:10
  66.5 2.1 multiply_reduce_fusion.1
  68.6 11.9 %while.36 = (s32[]{:T(128)}, bf16[2,512,2048]{2,1,0:T(8,128)(2,1)}, f32[1,2048]{1,0:T(1,128)S(1)}, bf16[2,512,512]{2,1,0:T(8,128)(2,1)}, f32[2048]{0:T(1024)S(1)}, /*index=5*/bf16[2048,512]{1,0:T(8,128)(2,1)}, s32[]{:T(128)}) while((s32[]{:T(128)}, bf16[2,512,2048]{2,1,0:T(8,128)(2,1)}, f32[1,2048]{1,0:T(1,128)S(1)}, ...), condition=%wide.region_3.4_spmd, body=%wide.region_1.3_spmd.sunk | while | flops 1080819200 | bytes 5264465 | solution.py:30
  68.6 1.2 multiply_reduce_fusion.3
  69.8 4.7 %fusion.33 = bf16[2,512,2048]{2,1,0:T(8,128)(2,1)} fusion(bf16[2,512,2048]{2,1,0:T(8,128)(2,1)} %get-tuple-element.330, s32[]{:T(128)} %get-tuple-element.329, bf16[2048,512]{1,0:T(8,128)(2,1)} %get-tuple-element.341, f32[2048]{0:T(1024)S(1)} %get-tuple-element.340, f32[512]{0:T(512)S(1)} %multiply_reduce_fusion.3, f32[2048]{0:T(1024)S(1)} %bitcast.62, ...), kind=kOutput, calls=%fused_computation.2.clone.1 | convolution fusion | flops 1080033280 | bytes 4738048 | tf_op jit(solution)/shard_map/while/body/eval_jaxpr/dot_general | solution.py:24
  74.5 1.2 multiply_reduce_fusion.3
  75.7 4.7 %fusion.33 = bf16[2,512,2048]{2,1,0:T(8,128)(2,1)} fusion(bf16[2,512,2048]{2,1,0:T(8,128)(2,1)} %get-tuple-element.330, s32[]{:T(128)} %get-tuple-element.329, bf16[2048,512]{1,0:T(8,128)(2,1)} %get-tuple-element.341, f32[2048]{0:T(1024)S(1)} %get-tuple-element.340, f32[512]{0:T(512)S(1)} %multiply_reduce_fusion.3, f32[2048]{0:T(1024)S(1)} %bitcast.62, ...), kind=kOutput, calls=%fused_computation.2.clone.1 | convolution fusion | flops 1080033280 | bytes 4738048 | tf_op jit(solution)/shard_map/while/body/eval_jaxpr/dot_general | solution.py:24
  80.5 0.0 copy-start.3
  80.5 4.5 %fusion.17 = f32[1024,128]{1,0:T(8,128)} fusion(bf16[1024,2048]{1,0:T(8,128)(2,1)} %bitcast.58, bf16[2048,128]{1,0:T(8,128)(2,1)} %all_gather.11), kind=kOutput, calls=%fused_computation.29 | convolution fusion | flops 536870912 | bytes 5242880 | tf_op jit(solution)/shard_map/dot_general | solution.py:31
  85.0 0.0 all-reduce.3.cloned.1.call-update
  85.0 0.0 reduce-scatter.3.cloned.1.call-start
  85.1 32.1 %all-reduce.3.cloned.1.call-done = f32[1024,128]{1,0:T(8,128)} async-done(((f32[1024,128]{1,0:T(8,128)}), f32[1024,128]{1,0:T(8,128)}) %all-reduce.3.cloned.1.call-update) | async-done | bytes 524304 | tf_op jit(solution)/shard_map/psum | solution.py:34
  117.1 0.0 copy-done.3
  117.1 0.0 copy-done.4
  117.1 0.0 copy-done.6
  117.1 1.2 multiply_convert_fusion
  118.3 0.0 copy-done.1
  118.3 13.7 %while.37 = (s32[]{:T(128)}, f32[2048,512]{1,0:T(8,128)}, f32[2048]{0:T(1024)S(1)}, bf16[2,512,2048]{2,1,0:T(8,128)(2,1)}, bf16[2,512,128]{2,1,0:T(8,128)(2,1)S(...) while((s32[]{:T(128)}, f32[2048,512]{1,0:T(8,128)}, ...), condition=%wide.region_7.8_spmd.clone, body=%wide.region_5.7_spmd.clone.sunk | while | flops 1349519360 | bytes 15893612 | solution.py:74
  118.3 2.5 %convert_reduce_fusion.2 = (f32[2048]{0:T(1024)S(1)}, bf16[512,2048]{1,0:T(8,128)(2,1)S(1)}) fusion(bf16[2048,128]{1,0:T(8,128)(2,1)} %get-tuple-element.366, bf16[2,512,128]{2,1,0:T(8,128)(2,1)S(1)} %get-tuple-element.365, s32[]{:T(128)} %get-tuple-element.352, bf16[2,512,2048]{2,1,0:T(8,128)(2,1)} %get-tuple-element.364), kind=kOutput, calls=%fused_computation.10.clone.1 | convolution fusion | flops 273676288 | bytes 4858880 | tf_op jit(solution)/shard_map/while/body/eval_jaxpr/dot_general | solution.py:47
  120.8 3.2 %select_add_fusion.4 = f32[2048,512]{1,0:T(8,128)} fusion(f32[2048,512]{1,0:T(8,128)} %get-tuple-element.353, bf16[512,2048]{1,0:T(8,128)(2,1)S(1)} %get-tuple-element.316, pred[]{:T(512)S(6)} %compare.6, bf16[2,512,512]{2,1,0:T(8,128)(2,1)S(1)} %get-tuple-element.367, s32[]{:T(128)} %get-tuple-element.352), kind=kOutput, calls=%fused_computation.9.clone.1 | convolution fusion | flops 1075838976 | bytes 11010053 | tf_op jit(solution)/shard_map/while/body/eval_jaxpr/dot_general | solution.py:52
  124.1 2.5 %convert_reduce_fusion.2 = (f32[2048]{0:T(1024)S(1)}, bf16[512,2048]{1,0:T(8,128)(2,1)S(1)}) fusion(bf16[2048,128]{1,0:T(8,128)(2,1)} %get-tuple-element.366, bf16[2,512,128]{2,1,0:T(8,128)(2,1)S(1)} %get-tuple-element.365, s32[]{:T(128)} %get-tuple-element.352, bf16[2,512,2048]{2,1,0:T(8,128)(2,1)} %get-tuple-element.364), kind=kOutput, calls=%fused_computation.10.clone.1 | convolution fusion | flops 273676288 | bytes 4858880 | tf_op jit(solution)/shard_map/while/body/eval_jaxpr/dot_general | solution.py:47
  126.6 5.4 %select_add_fusion.4 = f32[2048,512]{1,0:T(8,128)} fusion(f32[2048,512]{1,0:T(8,128)} %get-tuple-element.353, bf16[512,2048]{1,0:T(8,128)(2,1)S(1)} %get-tuple-element.316, pred[]{:T(512)S(6)} %compare.6, bf16[2,512,512]{2,1,0:T(8,128)(2,1)S(1)} %get-tuple-element.367, s32[]{:T(128)} %get-tuple-element.352), kind=kOutput, calls=%fused_computation.9.clone.1 | convolution fusion | flops 1075838976 | bytes 11010053 | tf_op jit(solution)/shard_map/while/body/eval_jaxpr/dot_general | solution.py:52
  132.0 0.0 reduce-scatter.3.cloned.1.call-update
  132.1 0.0 reduce-scatter.5.cloned.1.call-start
  132.1 0.0 copy-start.7
  132.1 0.0 copy-start.5
  132.1 0.0 copy-start.2
  132.2 5.4 %while.38 = (s32[]{:T(128)}, f32[2048,128]{1,0:T(8,128)S(1)}, bf16[2,512,2048]{2,1,0:T(8,128)(2,1)}, bf16[2,512,128]{2,1,0:T(8,128)(2,1)S(1)}, s32[]{:T(128)}, /*index=5*/s32[]{:T(128)}) while((s32[]{:T(128)}, f32[2048,128]{1,0:T(8,128)S(1)}, bf16[2,512,2048]{2,1,0:T(8,128)(2,1)}, bf16[2,512,128]{2,1,0:T(8,128)(2,1)S(1)}, ...), condition=%wide.region_11.12_spmd.clone, body=%wide.region_10.11_spmd.clone.sunk | while | flops 268959744 | bytes 4326479 | solution.py:65
  132.2 2.7 %convolution_add_fusion.2 = f32[2048,128]{1,0:T(8,128)S(1)} fusion(bf16[2,512,2048]{2,1,0:T(8,128)(2,1)} %get-tuple-element.384, s32[]{:T(128)} %get-tuple-element.376, f32[2048,128]{1,0:T(8,128)S(1)} %get-tuple-element.377, pred[]{:T(512)S(6)} %compare.7, bf16[2,512,128]{2,1,0:T(8,128)(2,1)S(1)} %get-tuple-element.385), kind=kOutput, calls=%fused_computation.18.clone.1 | convolution fusion | flops 268959744 | bytes 4326401 | tf_op jit(solution)/shard_map/while/body/eval_jaxpr/dot_general | solution.py:42
  134.9 2.6 %convolution_add_fusion.2 = f32[2048,128]{1,0:T(8,128)S(1)} fusion(bf16[2,512,2048]{2,1,0:T(8,128)(2,1)} %get-tuple-element.384, s32[]{:T(128)} %get-tuple-element.376, f32[2048,128]{1,0:T(8,128)S(1)} %get-tuple-element.377, pred[]{:T(512)S(6)} %compare.7, bf16[2,512,128]{2,1,0:T(8,128)(2,1)S(1)} %get-tuple-element.385), kind=kOutput, calls=%fused_computation.18.clone.1 | convolution fusion | flops 268959744 | bytes 4326401 | tf_op jit(solution)/shard_map/while/body/eval_jaxpr/dot_general | solution.py:42
  137.5 0.0 copy-start
  137.6 1.0 copy-done
  138.5 0.0 reduce-scatter.5.cloned.1.call-update
  138.5 0.0 copy-done.7
  138.6 0.6 dynamic-slice
  139.8 0.0 copy-done.5
  139.8 12.4 %all-reduce = f32[2048]{0:T(1024)S(1)} all-reduce(f32[2048]{0:T(1024)S(1)} %get-tuple-element.136), channel_id=3, replica_groups=mesh['groups'=2,'points'=4,'centers'=4] {'points'}, use_global_device_ids=true, to_apply=%region_9.10.clone | all-reduce | flops 2048 | bytes 16384
  152.2 0.1 dynamic-slice.1
  152.3 57.2 %reduce-scatter.3.cloned.1.call-done = f32[512,512]{1,0:T(8,128)} async-done(((f32[2048,512]{1,0:T(8,128)}), f32[512,512]{1,0:T(8,128)}) %reduce-scatter.3.cloned.1.call-update) | async-done | bytes 1048592 | tf_op jit(solution)/shard_map/reduce_scatter | solution.py:78
  209.5 0.0 copy-done.2
  209.5 2.4 subtract_multiply_fusion
  211.9 28.1 %reduce-scatter.5.cloned.1.call-done = f32[512,128]{1,0:T(8,128)} async-done(((f32[2048,128]{1,0:T(8,128)}), f32[512,128]{1,0:T(8,128)}) %reduce-scatter.5.cloned.1.call-update) | async-done | bytes 262160 | tf_op jit(solution)/shard_map/reduce_scatter | solution.py:66
  (11 shorter events, 0.0 us)
Async XLA Ops:
  7.2 59.4 %all-gather.3.cloned.1.call-start = ((), (), s32[]{:S(2)}) async-start(), calls=%async_computation.2 | async-start | bytes 2621440 | tf_op jit(solution)/shard_map/all_gather | solution.py:10
  7.9 109.2 %all-reduce.3.cloned.1.call-start = ((), (), s32[]{:S(2)}) async-start(), calls=%async_computation.3 | async-start | bytes 1048576 | tf_op jit(solution)/shard_map/psum | solution.py:34
  80.5 36.7 %copy-start.3 = (f32[1024,128]{1,0:T(8,128)S(1)}, f32[1024,128]{1,0:T(8,128)}, u32[]{:S(2)}) copy-start(f32[1024,128]{1,0:T(8,128)} %param.15) | copy-start | bytes 1572868
  80.5 36.7 %copy-start.4 = (f32[1024,128]{1,0:T(8,128)S(1)}, f32[1024,128]{1,0:T(8,128)}, u32[]{:S(2)}) copy-start(f32[1024,128]{1,0:T(8,128)} %param.14) | copy-start | bytes 1572868
  80.5 36.7 %copy-start.6 = (f32[128]{0:T(128)S(1)}, f32[128]{0:T(128)}, u32[]{:S(2)}) copy-start(f32[128]{0:T(128)} %param.16) | copy-start | bytes 1540
  80.5 37.8 %copy-start.1 = (bf16[2,512,512]{2,1,0:T(8,128)(2,1)S(1)}, bf16[2,512,512]{2,1,0:T(8,128)(2,1)}, u32[]{:S(2)}) copy-start(bf16[2,512,512]{2,1,0:T(8,128)(2,1)} %get-tuple-element.397) | copy-start | bytes 3145732
  85.0 124.5 %reduce-scatter.3.cloned.1.call-start = ((), (), s32[]{:S(2)}) async-start(), calls=%async_computation.4 | async-start | bytes 5242880 | tf_op jit(solution)/shard_map/reduce_scatter | solution.py:78
  132.1 108.0 %reduce-scatter.5.cloned.1.call-start = ((), (), s32[]{:S(2)}) async-start(), calls=%async_computation.5 | async-start | bytes 1310720 | tf_op jit(solution)/shard_map/reduce_scatter | solution.py:66
  132.1 6.4 %copy-start.7 = (u32[32]{0:T(128)S(1)}, u32[32]{0:T(128)}, u32[]{:S(2)}) copy-start(u32[32]{0:T(128)} %constant.66) | copy-start | bytes 388
  132.1 7.7 %copy-start.5 = (bf16[512]{0:T(512)(128)(2,1)S(1)}, bf16[512]{0:T(512)(128)(2,1)}, u32[]{:S(2)}) copy-start(bf16[512]{0:T(512)(128)(2,1)} %param.19) | copy-start | bytes 3076
  132.1 77.4 %copy-start.2 = (bf16[512,512]{1,0:T(8,128)(2,1)S(1)}, bf16[512,512]{1,0:T(8,128)(2,1)}, u32[]{:S(2)}) copy-start(bf16[512,512]{1,0:T(8,128)(2,1)} %param.17) | copy-start | bytes 1572868
  137.5 1.0 copy-start
Sparse Core Ops, SparseCore 0:
  9.6 56.9 all-gather.2
  85.1 31.9 all-reduce.2
  132.2 77.2 reduce-scatter.2
  212.3 27.6 reduce-scatter.4
where the time goes:
time: 247 us
  waiting for transfers between devices  140 us (57%)
  blocking collectives  47.9 us (19%)
  matrix products  32.9 us (13%)
  between operations  14.6 us (6%)
  other arithmetic  8.14 us (3%)
    reduce_scatter x1, waiting for transfers between devices, per_device(): lax.psum_scatter(moment_acc, 'points', scatter_dimension=0, tiled=True)  57.2 us
    psum x1, waiting for transfers between devices, per_device(): panel_pred = lax.psum(partial_pred, 'centers')  32.1 us
    reduce_scatter x1, waiting for transfers between devices, per_device(): lax.psum_scatter(coef_acc, 'points', scatter_dimension=0, tiled=True)  28.1 us
    all_gather x1, waiting for transfers between devices, per_device(): lax.all_gather(center_pos, 'points', axis=0, tiled=True)  22.4 us
    all_gather x1, blocking collectives, per_device(): lax.all_gather(coefficients, 'points', axis=0, tiled=True)  22 us
    all_gather x1, blocking collectives, per_device(): lax.all_gather(spread, 'points', axis=0, tiled=True)  13.5 us
    unnamed x1, blocking collectives  12.4 us
    dot_general x2, matrix products, kernel_of(): lax.dot_general(row_block, whole_pos, (((1,), (1,)), ((), ())), preferred...  9.42 us
  transfers between devices with their start and end apart: 4, of which 4 were waited for; matrix products, arithmetic and copies ran while one was open for 4% of the time, Pallas kernels for 0%

commit v1 on v0

v1 whole, which is shorter than its diff:
```python
import jax
import jax.numpy as jnp
from jax import lax
from jax.sharding import PartitionSpec as P


def per_device(train_points, saved_preds, targets, huber_delta, center_pos, coefficients, spread):
    n_points, in_width = train_points.shape
    n_cen = lax.axis_size("centers")
    own_rows = n_points // n_cen
    both = ("points", "centers")
    points = lax.all_gather(train_points, "points", axis=0, tiled=True)
    rates = spread.astype(jnp.float32)
    center_sq = jnp.sum(jnp.square(center_pos.astype(jnp.float32)), axis=1)
    point_sq = jnp.sum(jnp.square(points.astype(jnp.float32)), axis=1)
    cross = lax.dot_general(
        points, center_pos, (((1,), (1,)), ((), ())), preferred_element_type=jnp.float32
    )
    dist = point_sq[:, None] + center_sq[None, :] - 2.0 * cross
    kernel = jnp.exp(-rates[None, :] * dist / in_width).astype(jnp.bfloat16)
    partial_pred = jnp.dot(kernel, coefficients, preferred_element_type=jnp.float32)
    pred = lax.psum_scatter(partial_pred, both, scatter_dimension=0, tiled=True)
    first = lax.axis_index("centers") * own_rows
    saved = lax.dynamic_slice_in_dim(saved_preds, first, own_rows)
    target = lax.dynamic_slice_in_dim(targets, first, own_rows)
    residual = pred + saved - target
    own_cot = (residual / jnp.sqrt(1.0 + jnp.square(residual / huber_delta[None, :]))).astype(
        jnp.bfloat16
    )
    cotangent = lax.all_gather(own_cot, both, axis=0, tiled=True)
    grad_coef = lax.dot_general(
        kernel, cotangent, (((0,), (0,)), ((), ())), preferred_element_type=jnp.float32
    )
    mixing = lax.dot_general(
        cotangent, coefficients, (((1,), (1,)), ((), ())), preferred_element_type=jnp.float32
    )
    weights = (kernel.astype(jnp.float32) * mixing).astype(jnp.bfloat16)
    totals = jnp.sum(weights.astype(jnp.float32), axis=0)
    moment = lax.dot_general(
        weights, points, (((0,), (0,)), ((), ())), preferred_element_type=jnp.float32
    )
    grad_centers = (2.0 * rates / in_width)[:, None] * (
        moment - totals[:, None] * center_pos.astype(jnp.float32)
    )
    return (grad_centers, grad_coef)


def solution(mesh):
    rows = P(("groups", "points"), None)
    owned = P(("groups", "points", "centers"), None)
    return jax.shard_map(
        per_device,
        mesh=mesh,
        in_specs=(rows, rows, rows, P("groups"), owned, owned, P(("groups", "points", "centers"))),
        out_specs=(owned, owned),
        check_vma=False,
    )
```

time: 247 us -> 222 us (0.90)
  blocking collectives: 47.9 us -> 0 us
  waiting for transfers between devices: 140 us -> 182 us
  matrix products: 32.9 us -> 15.5 us
    all_gather x1 -> x2, waiting for transfers between devices: 22.4 us -> 121 us  [the longest x1 83.2 us: per_device(): points = lax.all_gather(train_points, 'points', axis=0, tiled=True)]
    all_gather x2 -> x0, blocking collectives: 35.5 us -> none  [the longest x1 22 us: per_device(): lax.all_gather(coefficients, 'points', axis=0, tiled=True)]
    psum x1 -> x0, waiting for transfers between devices: 32.1 us -> none  [per_device(): panel_pred = lax.psum(partial_pred, 'centers')]
    reduce_scatter x2 -> x1, waiting for transfers between devices: 85.3 us -> 60.2 us  [per_device(): pred = lax.psum_scatter(partial_pred, both, scatter_dimension=0, tiled=True)]
    dot_general x9 -> x5, matrix products: 32.9 us -> 15.5 us  [the longest x1 4.62 us: per_device(): lax.dot_general(kernel, cotangent, (((0,), (0,)), ((), ())), preferred_el...]
    unnamed x1 -> x0, blocking collectives: 12.4 us -> none
  transfers between devices with their start and end apart: 4 -> 3, of which waited for: 4 -> 3; matrix products, arithmetic and copies ran while one was open for 4% -> 1% of each run, Pallas kernels for 0% -> 0%
where the time goes in v1:
time: 222 us
  waiting for transfers between devices  182 us (82%)
  matrix products  15.5 us (7%)
  between operations  13.8 us (6%)
  other arithmetic  6.84 us (3%)
  local copies, waits for them, and re-layouts  3.12 us (1%)
    all_gather x1, waiting for transfers between devices, per_device(): points = lax.all_gather(train_points, 'points', axis=0, tiled=True)  83.2 us
    reduce_scatter x1, waiting for transfers between devices, per_device(): pred = lax.psum_scatter(partial_pred, both, scatter_dimension=0, tiled=True)  60.2 us
    all_gather x1, waiting for transfers between devices, per_device(): cotangent = lax.all_gather(own_cot, both, axis=0, tiled=True)  38.2 us
    dot_general x1, matrix products, per_device(): lax.dot_general(kernel, cotangent, (((0,), (0,)), ((), ())), preferred_el...  4.62 us
  transfers between devices with their start and end apart: 3, of which 3 were waited for; matrix products, arithmetic and copies ran while one was open for 1% of the time, Pallas kernels for 0%

profile of v1, /device:TPU:0, one launch (start us, length us, event | category | flops | bytes accessed | tf_op | source)
XLA Modules:
  0.0 221.7 jit_solution(10608579249660906500)
XLA Ops:
  7.2 0.0 copy-start
  7.2 0.0 copy-start.6
  7.2 0.0 all-gather.3.cloned.1.call-start
  7.2 0.7 all-gather.3.cloned.1.call-update
  7.9 0.0 reduce-scatter.2.cloned.1.call-start
  8.0 1.2 fusion.1
  9.2 0.7 convert_multiply_fusion.2
  9.9 83.2 %all-gather.3.cloned.1.call-done = bf16[4096,512]{1,0:T(8,128)(2,1)} async-done(((bf16[1024,512]{1,0:T(8,128)(2,1)}), bf16[4096,512]{1,0:T(8,128)(2,1)}) %all-gather.3.cloned.1.call-update) | async-done | bytes 4194320 | tf_op jit(solution)/shard_map/all_gather | solution.py:12
  93.1 0.0 copy-start.3
  93.1 3.2 %multiply_reduce_fusion = f32[4096]{0:T(1024)S(1)} fusion(bf16[4096,512]{1,0:T(8,128)(2,1)} %all-gather.3.cloned.1.call-done), kind=kLoop, calls=%fused_computation.3 | loop fusion | flops 6287360 | bytes 4210688 | tf_op jit(solution)/shard_map/reduce_sum | solution.py:15
  96.3 0.0 copy-done.6
  96.3 0.2 copy-done.3
  96.5 3.7 %exponential_convert_fusion = bf16[4096,512]{1,0:T(8,128)(2,1)S(1)} fusion(bf16[4096,512]{1,0:T(8,128)(2,1)S(1)} %copy-done.3, bf16[512,512]{1,0:T(8,128)(2,1)S(1)} %copy-done.6, f32[512]{0:T(512)S(1)} %fusion.1, f32[4096]{0:T(1024)S(1)} %multiply_reduce_fusion, f32[512]{0:T(512)S(1)} %get-tuple-element.3), kind=kOutput, calls=%fused_computation.2 | convolution fusion | flops 2160066560 | bytes 8933376 | tf_op jit(solution)/shard_map/dot_general | solution.py:16
  100.2 0.0 copy-start.1
  100.2 2.0 copy-done.1
  102.2 0.0 copy-done
  102.2 0.0 copy-start.7
  102.2 2.6 %fusion.2 = f32[4096,128]{1,0:T(8,128)} fusion(bf16[4096,512]{1,0:T(8,128)(2,1)S(1)} %exponential_convert_fusion, bf16[512,128]{1,0:T(8,128)(2,1)S(1)} %copy-done), kind=kOutput, calls=%fused_computation.12 | convolution fusion | flops 536870912 | bytes 6422528 | tf_op jit(solution)/shard_map/dot_general | solution.py:21
  104.8 0.0 reduce-scatter.2.cloned.1.call-update
  104.8 0.0 all-gather.5.cloned.1.call-start
  104.9 60.2 %reduce-scatter.2.cloned.1.call-done = f32[256,128]{1,0:T(8,128)} async-done(((f32[4096,128]{1,0:T(8,128)}), f32[256,128]{1,0:T(8,128)}) %reduce-scatter.2.cloned.1.call-update) | async-done | bytes 131088 | tf_op jit(solution)/shard_map/reduce_scatter | solution.py:22
  165.1 0.0 copy-done.7
  165.1 1.7 multiply_convert_fusion.1
  166.8 0.0 all-gather.5.cloned.1.call-update
  166.8 38.2 %all-gather.5.cloned.1.call-done = bf16[4096,128]{1,0:T(8,128)(2,1)} async-done(((bf16[256,128]{1,0:T(8,128)(2,1)}), bf16[4096,128]{1,0:T(8,128)(2,1)}) %all-gather.5.cloned.1.call-update) | async-done | bytes 1048592 | tf_op jit(solution)/shard_map/all_gather | solution.py:30
  205.0 0.0 copy-start.2
  205.0 0.0 copy-start.5
  205.0 4.6 %fusion.3 = f32[512,128]{1,0:T(8,128)} fusion(bf16[4096,512]{1,0:T(8,128)(2,1)} %copy-done.1, bf16[4096,128]{1,0:T(8,128)(2,1)} %all-gather.5.cloned.1.call-done), kind=kOutput, calls=%fused_computation.13 | convolution fusion | flops 536870912 | bytes 5505024 | tf_op jit(solution)/shard_map/dot_general | solution.py:31
  209.6 0.0 copy-done.2
  209.6 0.0 copy-done.5
  209.6 0.0 copy-start.4
  209.6 1.3 convert_reduce_fusion
  210.9 0.9 copy-done.4
  211.8 3.3 %fusion = f32[512,512]{1,0:T(8,128)} fusion(bf16[4096,512]{1,0:T(8,128)(2,1)S(1)} %get-tuple-element.5, bf16[4096,512]{1,0:T(8,128)(2,1)S(1)} %copy-done.4, bf16[512,512]{1,0:T(8,128)(2,1)S(1)} %copy-done.6, f32[512]{0:T(512)S(1)} %get-tuple-element.4, f32[512]{0:T(512)S(1)} %get-tuple-element.2), kind=kOutput, calls=%fused_computation.7 | convolution fusion | flops 2148532224 | bytes 9965568 | tf_op jit(solution)/shard_map/dot_general | solution.py:39
Async XLA Ops:
  7.2 95.0 %copy-start = (bf16[512,128]{1,0:T(8,128)(2,1)S(1)}, bf16[512,128]{1,0:T(8,128)(2,1)}, u32[]{:S(2)}) copy-start(bf16[512,128]{1,0:T(8,128)(2,1)} %param.12) | copy-start | bytes 393220
  7.2 89.2 %copy-start.6 = (bf16[512,512]{1,0:T(8,128)(2,1)S(1)}, bf16[512,512]{1,0:T(8,128)(2,1)}, u32[]{:S(2)}) copy-start(bf16[512,512]{1,0:T(8,128)(2,1)} %param.11) | copy-start | bytes 1572868
  7.2 85.9 %all-gather.3.cloned.1.call-start = ((), (), s32[]{:S(2)}) async-start(), calls=%async_computation.1 | async-start | bytes 5242880 | tf_op jit(solution)/shard_map/all_gather | solution.py:12
  7.9 157.1 %reduce-scatter.2.cloned.1.call-start = ((), (), s32[]{:S(2)}) async-start(), calls=%async_computation.2 | async-start | bytes 2228224 | tf_op jit(solution)/shard_map/reduce_scatter | solution.py:22
  93.1 3.4 %copy-start.3 = (bf16[4096,512]{1,0:T(8,128)(2,1)S(1)}, bf16[4096,512]{1,0:T(8,128)(2,1)}, u32[]{:S(2)}) copy-start(bf16[4096,512]{1,0:T(8,128)(2,1)} %all-gather.3.cloned.1.call-done) | copy-start | bytes 12582916
  100.2 2.0 copy-start.1
  102.2 62.9 %copy-start.7 = (f32[128]{0:T(128)S(1)}, f32[128]{0:T(128)}, u32[]{:S(2)}) copy-start(f32[128]{0:T(128)} %param.10) | copy-start | bytes 1540
  104.8 100.2 %all-gather.5.cloned.1.call-start = ((), (), s32[]{:S(2)}) async-start(), calls=%async_computation.3 | async-start | bytes 1114112 | tf_op jit(solution)/shard_map/all_gather | solution.py:30
  205.0 4.6 %copy-start.2 = (bf16[4096,512]{1,0:T(8,128)(2,1)S(1)}, bf16[4096,512]{1,0:T(8,128)(2,1)}, u32[]{:S(2)}) copy-start(bf16[4096,512]{1,0:T(8,128)(2,1)} %copy-done.1) | copy-start | bytes 12582916
  205.0 4.6 %copy-start.5 = (bf16[4096,128]{1,0:T(8,128)(2,1)S(1)}, bf16[4096,128]{1,0:T(8,128)(2,1)}, u32[]{:S(2)}) copy-start(bf16[4096,128]{1,0:T(8,128)(2,1)} %all-gather.5.cloned.1.call-done) | copy-start | bytes 3145732
  209.6 2.2 copy-start.4
Sparse Core Ops, SparseCore 0:
  9.6 83.4 all-gather.2
  105.0 60.0 reduce-scatter.1
  168.0 36.9 all-gather.4

commit v2 on v1

v2 whole, which is shorter than its diff:
```python
import functools

import jax
import jax.numpy as jnp
from jax import lax
from jax.experimental import pallas as pl
from jax.experimental.pallas import tpu as pltpu
from jax.sharding import PartitionSpec as P

CORES = 2
SUBS = 2
MESH = pl.DeviceIdType.MESH
f32, bf16 = jnp.float32, jnp.bfloat16


def body(Z, C, train, saved, target, delta, rates, cen, coef, gcen, gcoef,
         pts, kt, pred, pc, px, psum, pz, cot, cm2, coeft, csq, nrate, tot, sv, tg,
         zs, zr, xs, xr, cs, cr, pcs, pcr, pxs, pxr, pzs, pzr,
         czs, czr, cxs, cxr, ccs, ccr, ls):
    X = C // CORES
    q, width = pts.shape[2], pts.shape[3]
    sub = q // SUBS
    z, c = lax.axis_index("points"), lax.axis_index("centers")
    x, core = lax.div(c, CORES), lax.rem(c, CORES)
    other = 1 - core
    mate = x * CORES + other
    off = [lax.rem(x + k, X) for k in range(X)]
    back = [lax.rem(x + X - k, X) for k in range(X)]

    def remote(src, dst, ssem, rsem, **to):
        return pltpu.make_async_remote_copy(
            src_ref=src, dst_ref=dst, send_sem=ssem, recv_sem=rsem, device_id=to,
            device_id_type=MESH)

    def lane(xi, co):
        return xi * CORES + co

    def zcopy(way, b, s, own=False):
        rows = pl.ds(s * sub, sub)
        dst = pts.at[b, c, rows]
        src = train.at[c, rows] if own else dst
        to = z + 1 if way == 0 else z - 1
        return remote(src, dst, zs.at[way, b, s], zr.at[b, s], points=to)

    def xcopy(b, k, s, coming=False):
        li = lane(back[k], core) if coming else c
        ref = pts.at[b, li, pl.ds(s * sub, sub)]
        return remote(ref, ref, xs.at[b, k, s], xr.at[b, k, s], centers=lane(off[k], core))

    def ccopy(b, xi, s, coming=False):
        ref = pts.at[b, lane(xi, other if coming else core), pl.ds(s * sub, sub)]
        return remote(ref, ref, cs.at[b, xi, s], cr.at[b, xi, s], centers=mate)

    def pccopy(b):
        return remote(pred.at[b, other], pc.at[b], pcs.at[b], pcr.at[b], centers=mate)

    def pxcopy(b, k):
        return remote(pred.at[b, core, off[k]], px.at[b, k], pxs.at[b, k], pxr.at[b, k],
                      centers=lane(off[k], core))

    def pzcopy(b, src_z):
        return remote(psum.at[b], pz.at[src_z], pzs.at[b], pzr.at[src_z], points=b)

    def czcopy(b, to):
        ref = cot.at[b, core, x]
        return remote(ref, ref, czs.at[to], czr.at[b], points=to)

    def cxcopy(b, k, coming=False):
        ref = cot.at[b, core, back[k] if coming else x]
        return remote(ref, ref, cxs.at[b, k], cxr.at[b, k], centers=lane(off[k], core))

    def cccopy(b, xi, coming=False):
        ref = cot.at[b, other if coming else core, xi]
        return remote(ref, ref, ccs.at[b, xi], ccr.at[b, xi], centers=mate)

    def blocks(d, f, first=1):
        @pl.when((d >= first) & (d < Z) & (z - d >= 0))
        def _():
            f(z - d)

        @pl.when((d >= max(first, 1)) & (d < Z) & (z + d < Z))
        def _():
            f(z + d)

    barrier = pltpu.get_barrier_semaphore()
    for k in range(1, Z):
        pl.semaphore_signal(barrier, inc=1, device_id={"points": lax.rem(z + k, Z)},
                            device_id_type=MESH)
    for k in range(1, X):
        pl.semaphore_signal(barrier, inc=1, device_id={"centers": lane(off[k], core)},
                            device_id_type=MESH)
    pl.semaphore_signal(barrier, inc=1, device_id={"centers": mate}, device_id_type=MESH)
    own_points = pltpu.make_async_copy(train, pts.at[z], ls.at[0])
    own_saved = pltpu.make_async_copy(saved.at[c], sv, ls.at[1])
    own_target = pltpu.make_async_copy(target.at[c], tg, ls.at[2])
    own_points.start()
    own_saved.start()
    own_target.start()
    pl.semaphore_wait(barrier, Z - 1 + X - 1 + 1)

    for s in range(SUBS):
        @pl.when(z + 1 < Z)
        def _():
            zcopy(0, z, s, own=True).start()

        @pl.when(z > 0)
        def _():
            zcopy(1, z, s, own=True).start()

    n_cen = cen.shape[0]
    cen32 = cen[...].astype(f32)
    cm2[...] = (-2.0 * cen32).astype(bf16)
    coeft[...] = coef[...].astype(f32).T.astype(bf16)
    csq[...] = jnp.broadcast_to(jnp.sum(cen32 * cen32, axis=1, keepdims=True), (n_cen, 128))
    nrate[...] = jnp.broadcast_to(rates[...] * (-1.0 / width), (128, n_cen)).T
    gcen[...] = jnp.zeros_like(gcen)
    gcoef[...] = jnp.zeros_like(gcoef)
    tot[...] = jnp.zeros_like(tot)

    def wide(col):
        return jnp.concatenate([col] * (q // 128), axis=1)

    def forward(b):
        def piece(t, carry):
            rows_t = pts[b, t].T
            r32 = rows_t.astype(f32)
            psq = jnp.sum(r32 * r32, axis=0, keepdims=True)
            cross = jnp.dot(cm2[...], rows_t, preferred_element_type=f32)
            dist = (psq + wide(csq[...])) + cross
            k = jnp.exp(wide(nrate[...]) * dist).astype(bf16)
            kt[b, t] = k
            pred[b, lax.rem(t, CORES), lax.div(t, CORES)] = jnp.dot(
                coeft[...], k, preferred_element_type=f32)
            return carry
        lax.fori_loop(0, C, piece, 0)

    def backward(b):
        def piece(t, carry):
            ct = cot[b, lax.rem(t, CORES), lax.div(t, CORES)]
            k = kt[b, t]
            mix = lax.dot_general(coef[...], ct, (((1,), (1,)), ((), ())),
                                  preferred_element_type=f32)
            w = (k.astype(f32) * mix).astype(bf16)
            w32 = w.astype(f32)
            part = w32[:, :128]
            for i in range(1, q // 128):
                part = part + w32[:, i * 128:(i + 1) * 128]
            tot[...] += part
            gcen[...] += jnp.dot(w, pts[b, t], preferred_element_type=f32)
            gcoef[...] += jnp.dot(k, ct, preferred_element_type=f32)
            return carry
        lax.fori_loop(0, C, piece, 0)

    def arrive(b, s):
        zcopy(0, b, s).wait_recv()

        @pl.when((b < z) & (z + 1 < Z))
        def _():
            zcopy(0, b, s).start()

        @pl.when((b > z) & (z > 0))
        def _():
            zcopy(1, b, s).start()
        for k in range(1, X):
            xcopy(b, k, s).start()
        ccopy(b, x, s).start()

    def cross_x(b):
        for s in range(SUBS):
            for k in range(1, X):
                xcopy(b, k, s, coming=True).wait_recv()
                ccopy(b, back[k], s).start()

    def add_core(b):
        pccopy(b).wait_recv()
        pred[b, core] += pc[b]
        for k in range(1, X):
            pxcopy(b, k).start()

    def add_plane(b):
        total = pred[b, core, x]
        for k in range(1, X):
            pxcopy(b, k).wait_recv()
            total = total + px[b, k]
        psum[b] = total

        @pl.when(b != z)
        def _():
            pzcopy(b, z).start()

    def work(b):
        for xi in range(X):
            for s in range(SUBS):
                ccopy(b, xi, s, coming=True).wait_recv()
        forward(b)
        pccopy(b).start()

    own_points.wait()
    forward(z)
    pccopy(z).start()

    def step(d, carry):
        for s in range(SUBS):
            blocks(d, lambda b: arrive(b, s))
        blocks(d - 1, add_core, 0)
        blocks(d, cross_x)
        blocks(d - 1, add_plane, 0)
        blocks(d, work)
        return carry
    lax.fori_loop(1, Z + 1, step, 0)

    total = psum[z]
    for k in range(1, Z):
        src = lax.rem(z + k, Z)
        pzcopy(src, src).wait_recv()
        total = total + pz[src]
    own_saved.wait()
    own_target.wait()
    residual = total.T + sv[...] - tg[...]
    ratio = residual / delta[...]
    cot[z, core, x] = (residual / jnp.sqrt(1.0 + ratio * ratio)).astype(bf16)
    for k in range(1, Z):
        czcopy(z, lax.rem(z + k, Z)).start()

    def spread_cot(b):
        for k in range(1, X):
            cxcopy(b, k).start()
        cccopy(b, x).start()

    def cot_arrive(b):
        czcopy(b, b).wait_recv()
        spread_cot(b)

    def cot_work(b):
        for k in range(1, X):
            cxcopy(b, k, coming=True).wait_recv()
            cccopy(b, back[k]).start()
        for xi in range(X):
            cccopy(b, xi, coming=True).wait_recv()
        backward(b)

    spread_cot(z)

    def cot_step(d, carry):
        blocks(d, cot_arrive)
        blocks(d - 1, cot_work, 0)
        return carry
    lax.fori_loop(1, Z + 1, cot_step, 0)

    row_totals = jnp.sum(tot[...], axis=1, keepdims=True)
    scale = -2.0 * nrate[...]
    scale = jnp.concatenate([scale] * (width // 128), axis=1)
    gcen[...] = scale * (gcen[...] - row_totals * cen[...].astype(f32))

    def drain(b, carry):
        for s in range(SUBS):
            @pl.when((b <= z) & (z + 1 < Z))
            def _():
                zcopy(0, b, s).wait_send()

            @pl.when((b >= z) & (z > 0))
            def _():
                zcopy(1, b, s).wait_send()

        @pl.when(b != z)
        def _():
            for s in range(SUBS):
                for k in range(1, X):
                    xcopy(b, k, s).wait_send()
                for xi in range(X):
                    ccopy(b, xi, s).wait_send()
            pzcopy(b, z).wait_send()
            czcopy(z, b).wait_send()
        pccopy(b).wait_send()
        for k in range(1, X):
            pxcopy(b, k).wait_send()
            cxcopy(b, k).wait_send()
        for xi in range(X):
            cccopy(b, xi).wait_send()
        return carry
    lax.fori_loop(0, Z, drain, 0)


def per_device(Z, C, train_points, saved_preds, targets, huber_delta, center_pos, coefficients, spread):
    n_points, width = train_points.shape
    n_cen, n_out = coefficients.shape
    X, q = C // CORES, n_points // C
    vm, anywhere = pl.BlockSpec(memory_space=pltpu.VMEM), pl.BlockSpec(memory_space=pl.ANY)
    dma = pltpu.SemaphoreType.DMA
    flops = 2 * Z * n_points * n_cen * (2 * width + 3 * n_out)
    return tuple(pl.pallas_call(
        functools.partial(body, Z, C),
        out_shape=(jax.ShapeDtypeStruct((n_cen, width), f32),
                   jax.ShapeDtypeStruct((n_cen, n_out), f32)),
        in_specs=[anywhere] * 3 + [vm] * 4,
        out_specs=(vm, vm),
        scratch_shapes=[
            pltpu.VMEM((Z, C, q, width), bf16),
            pltpu.VMEM((Z, C, n_cen, q), bf16),
            pltpu.VMEM((Z, CORES, X, n_out, q), f32),
            pltpu.VMEM((Z, X, n_out, q), f32),
            pltpu.VMEM((Z, X, n_out, q), f32),
            pltpu.VMEM((Z, n_out, q), f32),
            pltpu.VMEM((Z, n_out, q), f32),
            pltpu.VMEM((Z, CORES, X, q, n_out), bf16),
            pltpu.VMEM((n_cen, width), bf16),
            pltpu.VMEM((n_out, n_cen), bf16),
            pltpu.VMEM((n_cen, 128), f32),
            pltpu.VMEM((n_cen, 128), f32),
            pltpu.VMEM((n_cen, 128), f32),
            pltpu.VMEM((q, n_out), f32),
            pltpu.VMEM((q, n_out), f32),
            dma((2, Z, SUBS)), dma((Z, SUBS)),
            dma((Z, X, SUBS)), dma((Z, X, SUBS)),
            dma((Z, X, SUBS)), dma((Z, X, SUBS)),
            dma((Z,)), dma((Z,)),
            dma((Z, X)), dma((Z, X)),
            dma((Z,)), dma((Z,)),
            dma((Z,)), dma((Z,)),
            dma((Z, X)), dma((Z, X)),
            dma((Z, X)), dma((Z, X)),
            dma((3,)),
        ],
        compiler_params=pltpu.CompilerParams(
            collective_id=0, has_side_effects=True, vmem_limit_bytes=60 << 20),
        cost_estimate=pl.CostEstimate(
            flops=flops, bytes_accessed=4 << 20, transcendentals=Z * n_points * n_cen),
    )(train_points.reshape(C, q, width), saved_preds.reshape(C, q, n_out),
      targets.reshape(C, q, n_out), huber_delta.reshape(1, n_out),
      spread.astype(f32).reshape(1, n_cen), center_pos, coefficients))


def solution(mesh):
    rows = P(("groups", "points"), None)
    owned = P(("groups", "points", "centers"), None)
    return jax.shard_map(
        functools.partial(per_device, mesh.shape["points"], mesh.shape["centers"]),
        mesh=mesh,
        in_specs=(rows, rows, rows, P("groups"), owned, owned, P(("groups", "points", "centers"))),
        out_specs=(owned, owned),
        check_vma=False,
    )
```

time: 222 us -> 84.1 us (0.38)
  waiting for transfers between devices: 182 us -> 0 us
  Pallas kernels: 0 us -> 79 us
  matrix products: 15.5 us -> 0 us
  between operations: 13.8 us -> 0.66 us
  other arithmetic: 6.84 us -> 0.58 us
    all_gather x2 -> x0, waiting for transfers between devices: 121 us -> none  [the longest x1 83.2 us: per_device(): points = lax.all_gather(train_points, 'points', axis=0, tiled=True)]
    pallas_call x0 -> x1, Pallas kernels: none -> 79 us  [per_device(): pl.pallas_call(functools.partial(body, Z, C), out_shape=(jax.ShapeDtypeSt...]
    reduce_scatter x1 -> x0, waiting for transfers between devices: 60.2 us -> none  [per_device(): pred = lax.psum_scatter(partial_pred, both, scatter_dimension=0, tiled=True)]
    dot_general x5 -> x0, matrix products: 15.5 us -> none  [the longest x1 4.62 us: per_device(): lax.dot_general(kernel, cotangent, (((0,), (0,)), ((), ())), preferred_el...]
    reduce_sum x2 -> x0, other arithmetic: 4.45 us -> none  [the longest x1 3.23 us: per_device(): point_sq = jnp.sum(jnp.square(points.astype(jnp.float32)), axis=1)]
  transfers between devices with their start and end apart: 3 -> 0, of which waited for: 3 -> 0; matrix products, arithmetic and copies ran while one was open for 1% -> 0% of each run, Pallas kernels for 0% -> 0%
where the time goes in v2:
time: 84.1 us; the launch traced here: 83.9 us
  Pallas kernels  79 us (94%)
  local copies, waits for them, and re-layouts  3.68 us (4%)
    pallas_call x1, Pallas kernels, per_device(): pl.pallas_call(functools.partial(body, Z, C), out_shape=(jax.ShapeDtypeSt...  79 us
    unnamed x6, local copies, waits for them, and re-layouts  3.68 us

profile of v2, /device:TPU:0, one launch (start us, length us, event | category | flops | bytes accessed | tf_op | source)
XLA Modules:
  0.0 83.9 jit_solution(18113893188798343607)
XLA Ops:
  0.6 0.0 copy-start.1
  0.6 0.7 copy-done.1
  1.3 0.6 reshape.27
  1.9 79.0 %shard_map.86 = (f32[512,512]{1,0:T(8,128)}, f32[512,128]{1,0:T(8,128)}) custom-call(bf16[4,256,512]{2,1,0:T(8,128)(2,1)} %bitcast.6, f32[4,256,128]{2,1,0:T(8,128)} %bitcast.7, f32[4,256,128]{2,1,0:T(8,128)} %bitcast.8, f32[1,128]{1,0:T(1,128)} %bitcast.9, f32[1,512]{1,0:T(1,128)} %bitcast.5, bf16[512,512]{1,0:T(8,128)(2,1)} %cen.1, bf16[512,128]{1,0:T(8,128)(2,1)} %coef.1), custom_call_target="tpu_custom_call" | custom-call | flops 5905580032 | bytes 4194304 | tf_op jit(solution)/shard_map/pallas_call | solution.py:291
  80.9 0.0 copy-start
  80.9 2.3 %copy.11 = f32[512,512]{1,0:T(8,128)} copy(f32[512,512]{1,0:T(8,128)} %get-tuple-element.4) | data formatting | bytes 2097152
  83.2 0.0 copy-done
  83.2 0.7 copy.12
Async XLA Ops:
  0.6 0.7 copy-start.1
  80.9 2.3 %copy-start = (f32[512,128]{1,0:T(8,128)S(1)}, f32[512,128]{1,0:T(8,128)}, u32[]{:S(2)}) copy-start(f32[512,128]{1,0:T(8,128)} %get-tuple-element.5) | copy-start | bytes 786436

commit v3 on v2

--- a/solution.py
+++ b/solution.py
@@ -9,12 +9,13 @@
 
 CORES = 2
 SUBS = 2
+LOG2E = 1.4426950408889634
 MESH = pl.DeviceIdType.MESH
 f32, bf16 = jnp.float32, jnp.bfloat16
 
 
 def body(Z, C, train, saved, target, delta, rates, cen, coef, gcen, gcoef,
-         pts, kt, pred, pc, px, psum, pz, cot, cm2, coeft, csq, nrate, tot, sv, tg,
+         pts, kt, pred, pc, px, psum, pz, cot, cm2, coeft, csq, nrate, tot, wbuf, sv, tg,
          zs, zr, xs, xr, cs, cr, pcs, pcr, pxs, pxr, pzs, pzr,
          czs, czr, cxs, cxr, ccs, ccr, ls):
     X = C // CORES
@@ -51,8 +52,9 @@
         ref = pts.at[b, lane(xi, other if coming else core), pl.ds(s * sub, sub)]
         return remote(ref, ref, cs.at[b, xi, s], cr.at[b, xi, s], centers=mate)
 
-    def pccopy(b):
-        return remote(pred.at[b, other], pc.at[b], pcs.at[b], pcr.at[b], centers=mate)
+    def pccopy(b, xi):
+        return remote(pred.at[b, other, xi], pc.at[b, xi], pcs.at[b, xi], pcr.at[b, xi],
+                      centers=mate)
 
     def pxcopy(b, k):
         return remote(pred.at[b, core, off[k]], px.at[b, k], pxs.at[b, k], pxr.at[b, k],
@@ -62,15 +64,15 @@
         return remote(psum.at[b], pz.at[src_z], pzs.at[b], pzr.at[src_z], points=b)
 
     def czcopy(b, to):
-        ref = cot.at[b, core, x]
+        ref = cot.at[b, c]
         return remote(ref, ref, czs.at[to], czr.at[b], points=to)
 
     def cxcopy(b, k, coming=False):
-        ref = cot.at[b, core, back[k] if coming else x]
+        ref = cot.at[b, lane(back[k], core) if coming else c]
         return remote(ref, ref, cxs.at[b, k], cxr.at[b, k], centers=lane(off[k], core))
 
     def cccopy(b, xi, coming=False):
-        ref = cot.at[b, other if coming else core, xi]
+        ref = cot.at[b, lane(xi, other if coming else core)]
         return remote(ref, ref, ccs.at[b, xi], ccr.at[b, xi], centers=mate)
 
     def blocks(d, f, first=1):
@@ -112,7 +114,7 @@
     cm2[...] = (-2.0 * cen32).astype(bf16)
     coeft[...] = coef[...].astype(f32).T.astype(bf16)
     csq[...] = jnp.broadcast_to(jnp.sum(cen32 * cen32, axis=1, keepdims=True), (n_cen, 128))
-    nrate[...] = jnp.broadcast_to(rates[...] * (-1.0 / width), (128, n_cen)).T
+    nrate[...] = jnp.broadcast_to(rates[...] * (-LOG2E / width), (128, n_cen)).T
     gcen[...] = jnp.zeros_like(gcen)
     gcoef[...] = jnp.zeros_like(gcoef)
     tot[...] = jnp.zeros_like(tot)
@@ -121,35 +123,38 @@
         return jnp.concatenate([col] * (q // 128), axis=1)
 
     def forward(b):
-        def piece(t, carry):
+        def piece(co, xi):
+            t = lane(xi, co)
             rows_t = pts[b, t].T
             r32 = rows_t.astype(f32)
             psq = jnp.sum(r32 * r32, axis=0, keepdims=True)
             cross = jnp.dot(cm2[...], rows_t, preferred_element_type=f32)
             dist = (psq + wide(csq[...])) + cross
-            k = jnp.exp(wide(nrate[...]) * dist).astype(bf16)
-            kt[b, t] = k
-            pred[b, lax.rem(t, CORES), lax.div(t, CORES)] = jnp.dot(
-                coeft[...], k, preferred_element_type=f32)
-            return carry
-        lax.fori_loop(0, C, piece, 0)
+            k = jnp.exp2(wide(nrate[...]) * dist).astype(bf16)
+            kt[b, :, pl.ds(pl.multiple_of(t * q, q), q)] = k
+            pred[b, co, xi] = jnp.dot(coeft[...], k, preferred_element_type=f32)
+        order = [off[k] for k in range(1, X)] + [x]
+        for xi in order:
+            piece(other, xi)
+            pccopy(b, xi).start()
+        for xi in order:
+            piece(core, xi)
 
     def backward(b):
-        def piece(t, carry):
-            ct = cot[b, lax.rem(t, CORES), lax.div(t, CORES)]
-            k = kt[b, t]
-            mix = lax.dot_general(coef[...], ct, (((1,), (1,)), ((), ())),
+        for t in range(C):
+            cols = slice(t * q, (t + 1) * q)
+            mix = lax.dot_general(coef[...], cot[b, t], (((1,), (1,)), ((), ())),
                                   preferred_element_type=f32)
-            w = (k.astype(f32) * mix).astype(bf16)
+            w = (kt[b, :, cols].astype(f32) * mix).astype(bf16)
             w32 = w.astype(f32)
             part = w32[:, :128]
             for i in range(1, q // 128):
                 part = part + w32[:, i * 128:(i + 1) * 128]
             tot[...] += part
-            gcen[...] += jnp.dot(w, pts[b, t], preferred_element_type=f32)
-            gcoef[...] += jnp.dot(k, ct, preferred_element_type=f32)
-            return carry
-        lax.fori_loop(0, C, piece, 0)
+            wbuf[:, cols] = w
+        gcen[...] += jnp.dot(wbuf[...], pts[b].reshape(C * q, width), preferred_element_type=f32)
+        gcoef[...] += jnp.dot(kt[b], cot[b].reshape(C * q, cot.shape[3]),
+                              preferred_element_type=f32)
 
     def arrive(b, s):
         zcopy(0, b, s).wait_recv()
@@ -172,10 +177,12 @@
                 ccopy(b, back[k], s).start()
 
     def add_core(b):
-        pccopy(b).wait_recv()
-        pred[b, core] += pc[b]
-        for k in range(1, X):
+        for k in range(1, X):
+            pccopy(b, off[k]).wait_recv()
+            pred[b, core, off[k]] += pc[b, off[k]]
             pxcopy(b, k).start()
+        pccopy(b, x).wait_recv()
+        pred[b, core, x] += pc[b, x]
 
     def add_plane(b):
         total = pred[b, core, x]
@@ -193,21 +200,21 @@
             for s in range(SUBS):
                 ccopy(b, xi, s, coming=True).wait_recv()
         forward(b)
-        pccopy(b).start()
 
     own_points.wait()
     forward(z)
-    pccopy(z).start()
 
     def step(d, carry):
         for s in range(SUBS):
             blocks(d, lambda b: arrive(b, s))
-        blocks(d - 1, add_core, 0)
-        blocks(d, cross_x)
-        blocks(d - 1, add_plane, 0)
-        blocks(d, work)
+        pl.when(d == 1)(lambda: add_core(z))
+        blocks(d - 2, add_core)
+        blocks(d - 1, cross_x)
+        blocks(d - 1, work)
+        pl.when(d == 1)(lambda: add_plane(z))
+        blocks(d - 2, add_plane)
         return carry
-    lax.fori_loop(1, Z + 1, step, 0)
+    lax.fori_loop(1, Z + 2, step, 0)
 
     total = psum[z]
     for k in range(1, Z):
@@ -218,7 +225,7 @@
     own_target.wait()
     residual = total.T + sv[...] - tg[...]
     ratio = residual / delta[...]
-    cot[z, core, x] = (residual / jnp.sqrt(1.0 + ratio * ratio)).astype(bf16)
+    cot[z, c] = (residual / jnp.sqrt(1.0 + ratio * ratio)).astype(bf16)
     for k in range(1, Z):
         czcopy(z, lax.rem(z + k, Z)).start()
 
@@ -248,9 +255,7 @@
     lax.fori_loop(1, Z + 1, cot_step, 0)
 
     row_totals = jnp.sum(tot[...], axis=1, keepdims=True)
-    scale = -2.0 * nrate[...]
-    scale = jnp.concatenate([scale] * (width // 128), axis=1)
-    gcen[...] = scale * (gcen[...] - row_totals * cen[...].astype(f32))
+    gcen[...] -= row_totals * cen[...].astype(f32)
 
     def drain(b, carry):
         for s in range(SUBS):
@@ -271,7 +276,8 @@
                     ccopy(b, xi, s).wait_send()
             pzcopy(b, z).wait_send()
             czcopy(z, b).wait_send()
-        pccopy(b).wait_send()
+        for xi in range(X):
+            pccopy(b, xi).wait_send()
         for k in range(1, X):
             pxcopy(b, k).wait_send()
             cxcopy(b, k).wait_send()
@@ -288,7 +294,9 @@
     vm, anywhere = pl.BlockSpec(memory_space=pltpu.VMEM), pl.BlockSpec(memory_space=pl.ANY)
     dma = pltpu.SemaphoreType.DMA
     flops = 2 * Z * n_points * n_cen * (2 * width + 3 * n_out)
-    return tuple(pl.pallas_call(
+    rates = spread.astype(f32)
+    held = Z * n_points * (2 * width + 2 * n_cen + 12 * n_out) + (12 << 20)
+    moved, grad_coef = pl.pallas_call(
         functools.partial(body, Z, C),
         out_shape=(jax.ShapeDtypeStruct((n_cen, width), f32),
                    jax.ShapeDtypeStruct((n_cen, n_out), f32)),
@@ -296,24 +304,25 @@
         out_specs=(vm, vm),
         scratch_shapes=[
             pltpu.VMEM((Z, C, q, width), bf16),
-            pltpu.VMEM((Z, C, n_cen, q), bf16),
+            pltpu.VMEM((Z, n_cen, C * q), bf16),
             pltpu.VMEM((Z, CORES, X, n_out, q), f32),
             pltpu.VMEM((Z, X, n_out, q), f32),
             pltpu.VMEM((Z, X, n_out, q), f32),
             pltpu.VMEM((Z, n_out, q), f32),
             pltpu.VMEM((Z, n_out, q), f32),
-            pltpu.VMEM((Z, CORES, X, q, n_out), bf16),
+            pltpu.VMEM((Z, C, q, n_out), bf16),
             pltpu.VMEM((n_cen, width), bf16),
             pltpu.VMEM((n_out, n_cen), bf16),
             pltpu.VMEM((n_cen, 128), f32),
             pltpu.VMEM((n_cen, 128), f32),
             pltpu.VMEM((n_cen, 128), f32),
+            pltpu.VMEM((n_cen, C * q), bf16),
             pltpu.VMEM((q, n_out), f32),
             pltpu.VMEM((q, n_out), f32),
             dma((2, Z, SUBS)), dma((Z, SUBS)),
             dma((Z, X, SUBS)), dma((Z, X, SUBS)),
             dma((Z, X, SUBS)), dma((Z, X, SUBS)),
-            dma((Z,)), dma((Z,)),
+            dma((Z, X)), dma((Z, X)),
             dma((Z, X)), dma((Z, X)),
             dma((Z,)), dma((Z,)),
             dma((Z,)), dma((Z,)),
@@ -322,12 +331,13 @@
             dma((3,)),
         ],
         compiler_params=pltpu.CompilerParams(
-            collective_id=0, has_side_effects=True, vmem_limit_bytes=60 << 20),
+            collective_id=0, has_side_effects=True, vmem_limit_bytes=min(held, 60 << 20)),
         cost_estimate=pl.CostEstimate(
             flops=flops, bytes_accessed=4 << 20, transcendentals=Z * n_points * n_cen),
     )(train_points.reshape(C, q, width), saved_preds.reshape(C, q, n_out),
       targets.reshape(C, q, n_out), huber_delta.reshape(1, n_out),
-      spread.astype(f32).reshape(1, n_cen), center_pos, coefficients))
+      rates.reshape(1, n_cen), center_pos, coefficients)
+    return (2.0 * rates / width)[:, None] * moved, grad_coef
 
 
 def solution(mesh):

time: 84.1 us -> 76.6 us (0.911)
  Pallas kernels: 79 us -> 66.6 us
  local copies, waits for them, and re-layouts: 3.68 us -> 7.28 us
    pallas_call x1, Pallas kernels: 79 us -> 66.6 us  [per_device(): pl.pallas_call(functools.partial(body, Z, C), out_shape=(jax.ShapeDtypeSt...]
    unnamed x6 -> x15, local copies, waits for them, and re-layouts: 3.68 us -> 7.28 us
    mul x0 -> x1, other arithmetic: none -> 1.11 us  [per_device(): return ((2.0 * rates / width)[:, None] * moved, grad_coef)]
where the time goes in v3:
time: 76.6 us; the launch traced here: 75.7 us
  Pallas kernels  66.6 us (87%)
  local copies, waits for them, and re-layouts  7.28 us (10%)
  other arithmetic  1.11 us (1%)
    pallas_call x1, Pallas kernels, per_device(): pl.pallas_call(functools.partial(body, Z, C), out_shape=(jax.ShapeDtypeSt...  66.6 us
    unnamed x15, local copies, waits for them, and re-layouts  7.28 us

profile of v3, /device:TPU:0, one launch (start us, length us, event | category | flops | bytes accessed | tf_op | source)
XLA Modules:
  0.0 75.7 jit_solution(15281872295972808708)
XLA Ops:
  0.6 0.0 copy-start.6
  0.6 0.7 copy-done.6
  1.3 0.0 copy-start.5
  1.3 0.7 copy-done.5
  2.0 0.0 copy-start
  2.0 1.2 %copy-done = bf16[1024,512]{1,0:T(8,128)(2,1)S(1)} copy-done((bf16[1024,512]{1,0:T(8,128)(2,1)S(1)}, bf16[1024,512]{1,0:T(8,128)(2,1)}, u32[]{:S(2)}) %copy-start) | copy-done | bytes 1048600
  3.2 0.0 copy-start.1
  3.2 1.0 %copy-done.1 = f32[1024,128]{1,0:T(8,128)S(1)} copy-done((f32[1024,128]{1,0:T(8,128)S(1)}, f32[1024,128]{1,0:T(8,128)}, u32[]{:S(2)}) %copy-start.1) | copy-done | bytes 524312
  4.2 0.0 copy-start.2
  4.2 1.0 %copy-done.2 = f32[1024,128]{1,0:T(8,128)S(1)} copy-done((f32[1024,128]{1,0:T(8,128)S(1)}, f32[1024,128]{1,0:T(8,128)}, u32[]{:S(2)}) %copy-start.2) | copy-done | bytes 524312
  5.3 0.0 copy-start.3
  5.3 1.0 %copy-done.3 = bf16[512,512]{1,0:T(8,128)(2,1)S(1)} copy-done((bf16[512,512]{1,0:T(8,128)(2,1)S(1)}, bf16[512,512]{1,0:T(8,128)(2,1)}, u32[]{:S(2)}) %copy-start.3) | copy-done | bytes 524312
  6.3 0.0 copy-start.4
  6.3 0.9 %copy-done.4 = bf16[512,128]{1,0:T(8,128)(2,1)S(1)} copy-done((bf16[512,128]{1,0:T(8,128)(2,1)S(1)}, bf16[512,128]{1,0:T(8,128)(2,1)}, u32[]{:S(2)}) %copy-start.4) | copy-done | bytes 131096
  7.2 66.6 %shard_map.86 = (f32[512,512]{1,0:T(8,128)S(1)}, f32[512,128]{1,0:T(8,128)S(1)}) custom-call(bf16[4,256,512]{2,1,0:T(8,128)(2,1)S(1)} %bitcast.6, f32[4,256,128]{2,1,0:T(8,128)S(1)} %bitcast.7, f32[4,256,128]{2,1,0:T(8,128)S(1)} %bitcast.8, f32[1,128]{1,0:T(1,128)S(1)} %bitcast.9, f32[1,512]{1,0:T(1,128)S(1)} %bitcast.5, bf16[512,512]{1,0:T(8,128)(2,1)S(1)} %copy-done.3, ...), custom_call_target="tpu_custom_call" | custom-call | flops 5905580032 | bytes 4194304 | tf_op jit(solution)/shard_map/pallas_call | solution.py:299
  73.9 1.1 %broadcast_multiply_fusion = f32[512,512]{1,0:T(8,128)} fusion(f32[512,512]{1,0:T(8,128)S(1)} %get-tuple-element.4, f32[512]{0:T(512)S(1)} %broadcast_multiply_fusion.1), kind=kLoop, calls=%fused_computation | loop fusion | flops 262144 | bytes 2099200 | tf_op jit(solution)/shard_map/mul | solution.py:340
  75.0 0.7 copy.10
  (2 shorter events, 0.0 us)
Async XLA Ops:
  0.6 0.7 copy-start.6
  1.3 0.7 copy-start.5
  2.0 1.2 %copy-start = (bf16[1024,512]{1,0:T(8,128)(2,1)S(1)}, bf16[1024,512]{1,0:T(8,128)(2,1)}, u32[]{:S(2)}) copy-start(bf16[1024,512]{1,0:T(8,128)(2,1)} %param.7) | copy-start | bytes 3145732
  3.2 1.0 %copy-start.1 = (f32[1024,128]{1,0:T(8,128)S(1)}, f32[1024,128]{1,0:T(8,128)}, u32[]{:S(2)}) copy-start(f32[1024,128]{1,0:T(8,128)} %param.8) | copy-start | bytes 1572868
  4.2 1.0 %copy-start.2 = (f32[1024,128]{1,0:T(8,128)S(1)}, f32[1024,128]{1,0:T(8,128)}, u32[]{:S(2)}) copy-start(f32[1024,128]{1,0:T(8,128)} %param.9) | copy-start | bytes 1572868
  5.3 1.0 %copy-start.3 = (bf16[512,512]{1,0:T(8,128)(2,1)S(1)}, bf16[512,512]{1,0:T(8,128)(2,1)}, u32[]{:S(2)}) copy-start(bf16[512,512]{1,0:T(8,128)(2,1)} %cen.1) | copy-start | bytes 1572868
  6.3 0.9 %copy-start.4 = (bf16[512,128]{1,0:T(8,128)(2,1)S(1)}, bf16[512,128]{1,0:T(8,128)(2,1)}, u32[]{:S(2)}) copy-start(bf16[512,128]{1,0:T(8,128)(2,1)} %coef.1) | copy-start | bytes 393220

commit v4 on v3

--- a/solution.py
+++ b/solution.py
@@ -14,10 +14,11 @@
 f32, bf16 = jnp.float32, jnp.bfloat16
 
 
-def body(Z, C, train, saved, target, delta, rates, cen, coef, gcen, gcoef,
-         pts, kt, pred, pc, px, psum, pz, cot, cm2, coeft, csq, nrate, tot, wbuf, sv, tg,
-         zs, zr, xs, xr, cs, cr, pcs, pcr, pxs, pxr, pzs, pzr,
-         czs, czr, cxs, cxr, ccs, ccr, ls):
+def body(Z, C, train, saved, target, delta_in, rates_in, cen_in, coef_in, gcen, gcoef,
+         pts, ptst, psqs, kt, pred, pc, psum, pz, cot, cm2, coeft, csq, nrate, tot, wbuf, sv, tg,
+         delta, rates, cen, coef,
+         zs, zr, xs, xr, cs, cr, pcs, pcr, pzs, pzr,
+         czs, czr, cxs, cxr, ccs, ccr, es, er, ls):
     X = C // CORES
     q, width = pts.shape[2], pts.shape[3]
     sub = q // SUBS
@@ -52,13 +53,14 @@
         ref = pts.at[b, lane(xi, other if coming else core), pl.ds(s * sub, sub)]
         return remote(ref, ref, cs.at[b, xi, s], cr.at[b, xi, s], centers=mate)
 
-    def pccopy(b, xi):
-        return remote(pred.at[b, other, xi], pc.at[b, xi], pcs.at[b, xi], pcr.at[b, xi],
-                      centers=mate)
-
-    def pxcopy(b, k):
-        return remote(pred.at[b, core, off[k]], px.at[b, k], pxs.at[b, k], pxr.at[b, k],
-                      centers=lane(off[k], core))
+    def ecopies(k, coming=False):
+        at = back[k] if coming else x
+        return [remote(src, dst.at[at], es.at[k, i], er.at[k, i], centers=lane(off[k], core))
+                for i, (src, dst) in enumerate(
+                    ((cen_in, cen), (coef_in, coef), (rates_in, rates)))]
+
+    def pccopy(b):
+        return remote(pred.at[b, other], pc.at[b], pcs.at[b], pcr.at[b], centers=mate)
 
     def pzcopy(b, src_z):
         return remote(psum.at[b], pz.at[src_z], pzs.at[b], pzr.at[src_z], points=b)
@@ -98,6 +100,10 @@
     own_points.start()
     own_saved.start()
     own_target.start()
+    small = [pltpu.make_async_copy(a, b, ls.at[3 + i]) for i, (a, b) in enumerate(
+        ((cen_in, cen.at[x]), (coef_in, coef.at[x]), (rates_in, rates.at[x]), (delta_in, delta)))]
+    for copy in small:
+        copy.start()
     pl.semaphore_wait(barrier, Z - 1 + X - 1 + 1)
 
     for s in range(SUBS):
@@ -109,12 +115,22 @@
         def _():
             zcopy(1, z, s, own=True).start()
 
-    n_cen = cen.shape[0]
-    cen32 = cen[...].astype(f32)
-    cm2[...] = (-2.0 * cen32).astype(bf16)
-    coeft[...] = coef[...].astype(f32).T.astype(bf16)
-    csq[...] = jnp.broadcast_to(jnp.sum(cen32 * cen32, axis=1, keepdims=True), (n_cen, 128))
-    nrate[...] = jnp.broadcast_to(rates[...] * (-LOG2E / width), (128, n_cen)).T
+    for k in range(1, X):
+        for copy in ecopies(k):
+            copy.start()
+
+    n_cen = cen.shape[1]
+
+    def prepare(xi):
+        cen32 = cen[xi].astype(f32)
+        cm2[xi] = (-2.0 * cen32).astype(bf16)
+        coeft[xi] = coef[xi].astype(f32).T.astype(bf16)
+        csq[xi] = jnp.broadcast_to(jnp.sum(cen32 * cen32, axis=1, keepdims=True), (n_cen, 128))
+        nrate[xi] = jnp.broadcast_to(rates[xi] * (-LOG2E / width), (128, n_cen)).T
+
+    for copy in small:
+        copy.wait()
+    prepare(x)
     gcen[...] = jnp.zeros_like(gcen)
     gcoef[...] = jnp.zeros_like(gcoef)
     tot[...] = jnp.zeros_like(tot)
@@ -122,28 +138,51 @@
     def wide(col):
         return jnp.concatenate([col] * (q // 128), axis=1)
 
-    def forward(b):
-        def piece(co, xi):
-            t = lane(xi, co)
+    def cols_of(t):
+        return pl.ds(pl.multiple_of(t * q, q), q)
+
+    def square_sum(rows_t):
+        r32 = rows_t.astype(f32)
+        return jnp.sum(r32 * r32, axis=0, keepdims=True)
+
+    def kernel_of(rows_t, psq, xi):
+        cross = jnp.dot(cm2[xi], rows_t, preferred_element_type=f32)
+        dist = (psq + wide(csq[xi])) + cross
+        return jnp.exp2(wide(nrate[xi]) * dist).astype(bf16)
+
+    def forward_own(b):
+        for co in (other, core):
+            t = lane(x, co)
             rows_t = pts[b, t].T
-            r32 = rows_t.astype(f32)
-            psq = jnp.sum(r32 * r32, axis=0, keepdims=True)
-            cross = jnp.dot(cm2[...], rows_t, preferred_element_type=f32)
-            dist = (psq + wide(csq[...])) + cross
-            k = jnp.exp2(wide(nrate[...]) * dist).astype(bf16)
-            kt[b, :, pl.ds(pl.multiple_of(t * q, q), q)] = k
-            pred[b, co, xi] = jnp.dot(coeft[...], k, preferred_element_type=f32)
-        order = [off[k] for k in range(1, X)] + [x]
-        for xi in order:
-            piece(other, xi)
-            pccopy(b, xi).start()
-        for xi in order:
-            piece(core, xi)
+            psq = square_sum(rows_t)
+            ptst[b, co] = rows_t
+            psqs[b, co] = psq
+            k = kernel_of(rows_t, psq, x)
+            kt[b, :, cols_of(t)] = k
+            pred[b, co] = jnp.dot(coeft[x], k, preferred_element_type=f32)
+
+    def forward_rest(b):
+        for co in (other, core):
+            rows_t, psq = ptst[b, co], psqs[b, co]
+            total = pred[b, co]
+            for i in range(1, X):
+                k = kernel_of(rows_t, psq, off[i])
+                total = total + jnp.dot(coeft[off[i]], k, preferred_element_type=f32)
+            pred[b, co] = total
+            if co is other:
+                pccopy(b).start()
+
+    def kernel_rest(b):
+        for i in range(1, X):
+            for co in (core, other):
+                t = lane(back[i], co)
+                rows_t = pts[b, t].T
+                kt[b, :, cols_of(t)] = kernel_of(rows_t, square_sum(rows_t), x)
 
     def backward(b):
         for t in range(C):
             cols = slice(t * q, (t + 1) * q)
-            mix = lax.dot_general(coef[...], cot[b, t], (((1,), (1,)), ((), ())),
+            mix = lax.dot_general(coef[x], cot[b, t], (((1,), (1,)), ((), ())),
                                   preferred_element_type=f32)
             w = (kt[b, :, cols].astype(f32) * mix).astype(bf16)
             w32 = w.astype(f32)
@@ -166,55 +205,69 @@
         @pl.when((b > z) & (z > 0))
         def _():
             zcopy(1, b, s).start()
-        for k in range(1, X):
-            xcopy(b, k, s).start()
         ccopy(b, x, s).start()
 
-    def cross_x(b):
+    def arrivals(d):
+        for s in range(SUBS):
+            blocks(d, lambda b: arrive(b, s))
+
+    def send_x(b):
+        for s in range(SUBS):
+            for k in range(1, X):
+                xcopy(b, k, s).start()
+
+    def work(b):
+        for s in range(SUBS):
+            ccopy(b, x, s, coming=True).wait_recv()
+        forward_own(b)
+
+    def finish(b):
+        pccopy(b).wait_recv()
+        psum[b] = pred[b, core] + pc[b]
+
+        @pl.when(b != z)
+        def _():
+            pzcopy(b, z).start()
+
+    def rest(b):
         for s in range(SUBS):
             for k in range(1, X):
                 xcopy(b, k, s, coming=True).wait_recv()
                 ccopy(b, back[k], s).start()
-
-    def add_core(b):
-        for k in range(1, X):
-            pccopy(b, off[k]).wait_recv()
-            pred[b, core, off[k]] += pc[b, off[k]]
-            pxcopy(b, k).start()
-        pccopy(b, x).wait_recv()
-        pred[b, core, x] += pc[b, x]
-
-    def add_plane(b):
-        total = pred[b, core, x]
-        for k in range(1, X):
-            pxcopy(b, k).wait_recv()
-            total = total + px[b, k]
-        psum[b] = total
-
-        @pl.when(b != z)
-        def _():
-            pzcopy(b, z).start()
-
-    def work(b):
-        for xi in range(X):
-            for s in range(SUBS):
-                ccopy(b, xi, s, coming=True).wait_recv()
-        forward(b)
+        for s in range(SUBS):
+            for k in range(1, X):
+                ccopy(b, back[k], s, coming=True).wait_recv()
+        kernel_rest(b)
 
     own_points.wait()
-    forward(z)
-
-    def step(d, carry):
-        for s in range(SUBS):
-            blocks(d, lambda b: arrive(b, s))
-        pl.when(d == 1)(lambda: add_core(z))
-        blocks(d - 2, add_core)
-        blocks(d - 1, cross_x)
-        blocks(d - 1, work)
-        pl.when(d == 1)(lambda: add_plane(z))
-        blocks(d - 2, add_plane)
+    forward_own(z)
+    kernel_rest(z)
+
+    def early(d, carry):
+        arrivals(d)
+        blocks(d, work)
         return carry
-    lax.fori_loop(1, Z + 2, step, 0)
+    lax.fori_loop(1, Z - 1, early, 0)
+
+    for k in range(1, X):
+        for copy in ecopies(k, coming=True):
+            copy.wait_recv()
+        prepare(back[k])
+
+    def middle(d, carry):
+        @pl.when((d >= 1) & (d < Z - 1))
+        def _():
+            blocks(d, send_x)
+
+        @pl.when(d == Z - 1)
+        def _():
+            arrivals(d)
+            blocks(d, send_x)
+            blocks(d, work)
+        blocks(d, forward_rest, 0)
+        blocks(d - 1, finish, 0)
+        return carry
+    lax.fori_loop(0, Z + 1, middle, 0)
 
     total = psum[z]
     for k in range(1, Z):
@@ -238,24 +291,36 @@
         czcopy(b, b).wait_recv()
         spread_cot(b)
 
-    def cot_work(b):
+    def cot_cross(b):
         for k in range(1, X):
             cxcopy(b, k, coming=True).wait_recv()
             cccopy(b, back[k]).start()
+
+    def cot_work(b):
         for xi in range(X):
             cccopy(b, xi, coming=True).wait_recv()
         backward(b)
 
     spread_cot(z)
 
-    def cot_step(d, carry):
+    def late(d, carry):
+        blocks(d, rest)
         blocks(d, cot_arrive)
-        blocks(d - 1, cot_work, 0)
         return carry
-    lax.fori_loop(1, Z + 1, cot_step, 0)
+    lax.fori_loop(1, Z, late, 0)
+
+    cot_cross(z)
+
+    def last(d, carry):
+        blocks(d + 1, cot_cross)
+        blocks(d, cot_work, 0)
+        return carry
+    lax.fori_loop(0, Z, last, 0)
 
     row_totals = jnp.sum(tot[...], axis=1, keepdims=True)
-    gcen[...] -= row_totals * cen[...].astype(f32)
+    scale = (-2.0 / LOG2E) * nrate[x]
+    scale = jnp.concatenate([scale] * (width // 128), axis=1)
+    gcen[...] = scale * (gcen[...] - row_totals * cen[x].astype(f32))
 
     def drain(b, carry):
         for s in range(SUBS):
@@ -276,68 +341,71 @@
                     ccopy(b, xi, s).wait_send()
             pzcopy(b, z).wait_send()
             czcopy(z, b).wait_send()
-        for xi in range(X):
-            pccopy(b, xi).wait_send()
+        pccopy(b).wait_send()
         for k in range(1, X):
-            pxcopy(b, k).wait_send()
             cxcopy(b, k).wait_send()
         for xi in range(X):
             cccopy(b, xi).wait_send()
         return carry
     lax.fori_loop(0, Z, drain, 0)
+    for k in range(1, X):
+        for copy in ecopies(k):
+            copy.wait_send()
 
 
 def per_device(Z, C, train_points, saved_preds, targets, huber_delta, center_pos, coefficients, spread):
     n_points, width = train_points.shape
     n_cen, n_out = coefficients.shape
     X, q = C // CORES, n_points // C
-    vm, anywhere = pl.BlockSpec(memory_space=pltpu.VMEM), pl.BlockSpec(memory_space=pl.ANY)
+    vm, in_hbm = pl.BlockSpec(memory_space=pltpu.VMEM), pl.BlockSpec(memory_space=pltpu.HBM)
     dma = pltpu.SemaphoreType.DMA
     flops = 2 * Z * n_points * n_cen * (2 * width + 3 * n_out)
-    rates = spread.astype(f32)
-    held = Z * n_points * (2 * width + 2 * n_cen + 12 * n_out) + (12 << 20)
-    moved, grad_coef = pl.pallas_call(
+    return tuple(pl.pallas_call(
         functools.partial(body, Z, C),
         out_shape=(jax.ShapeDtypeStruct((n_cen, width), f32),
                    jax.ShapeDtypeStruct((n_cen, n_out), f32)),
-        in_specs=[anywhere] * 3 + [vm] * 4,
+        in_specs=[in_hbm] * 7,
         out_specs=(vm, vm),
         scratch_shapes=[
             pltpu.VMEM((Z, C, q, width), bf16),
+            pltpu.VMEM((Z, CORES, width, q), bf16),
+            pltpu.VMEM((Z, CORES, 1, q), f32),
             pltpu.VMEM((Z, n_cen, C * q), bf16),
-            pltpu.VMEM((Z, CORES, X, n_out, q), f32),
-            pltpu.VMEM((Z, X, n_out, q), f32),
-            pltpu.VMEM((Z, X, n_out, q), f32),
+            pltpu.VMEM((Z, CORES, n_out, q), f32),
+            pltpu.VMEM((Z, n_out, q), f32),
             pltpu.VMEM((Z, n_out, q), f32),
             pltpu.VMEM((Z, n_out, q), f32),
             pltpu.VMEM((Z, C, q, n_out), bf16),
-            pltpu.VMEM((n_cen, width), bf16),
-            pltpu.VMEM((n_out, n_cen), bf16),
-            pltpu.VMEM((n_cen, 128), f32),
-            pltpu.VMEM((n_cen, 128), f32),
+            pltpu.VMEM((X, n_cen, width), bf16),
+            pltpu.VMEM((X, n_out, n_cen), bf16),
+            pltpu.VMEM((X, n_cen, 128), f32),
+            pltpu.VMEM((X, n_cen, 128), f32),
             pltpu.VMEM((n_cen, 128), f32),
             pltpu.VMEM((n_cen, C * q), bf16),
             pltpu.VMEM((q, n_out), f32),
             pltpu.VMEM((q, n_out), f32),
+            pltpu.VMEM((1, n_out), f32),
+            pltpu.VMEM((X, 1, n_cen), f32),
+            pltpu.VMEM((X, n_cen, width), bf16),
+            pltpu.VMEM((X, n_cen, n_out), bf16),
             dma((2, Z, SUBS)), dma((Z, SUBS)),
             dma((Z, X, SUBS)), dma((Z, X, SUBS)),
             dma((Z, X, SUBS)), dma((Z, X, SUBS)),
-            dma((Z, X)), dma((Z, X)),
-            dma((Z, X)), dma((Z, X)),
+            dma((Z,)), dma((Z,)),
             dma((Z,)), dma((Z,)),
             dma((Z,)), dma((Z,)),
             dma((Z, X)), dma((Z, X)),
             dma((Z, X)), dma((Z, X)),
-            dma((3,)),
+            dma((X, 3)), dma((X, 3)),
+            dma((7,)),
         ],
         compiler_params=pltpu.CompilerParams(
-            collective_id=0, has_side_effects=True, vmem_limit_bytes=min(held, 60 << 20)),
+            collective_id=0, has_side_effects=True, vmem_limit_bytes=60 << 20),
         cost_estimate=pl.CostEstimate(
             flops=flops, bytes_accessed=4 << 20, transcendentals=Z * n_points * n_cen),
     )(train_points.reshape(C, q, width), saved_preds.reshape(C, q, n_out),
       targets.reshape(C, q, n_out), huber_delta.reshape(1, n_out),
-      rates.reshape(1, n_cen), center_pos, coefficients)
-    return (2.0 * rates / width)[:, None] * moved, grad_coef
+      spread.astype(f32).reshape(1, n_cen), center_pos, coefficients))
 
 
 def solution(mesh):

time: 76.6 us -> 60.6 us (0.79); the launches traced: 75.7 us -> 60.5 us
  Pallas kernels: 66.6 us -> 55.6 us
  local copies, waits for them, and re-layouts: 7.28 us -> 3.68 us
    pallas_call x1, Pallas kernels: 66.6 us -> 55.6 us  [per_device(): pl.pallas_call(functools.partial(body, Z, C), out_shape=(jax.ShapeDtypeSt...]
    unnamed x15 -> x6, local copies, waits for them, and re-layouts: 7.28 us -> 3.68 us
    mul x1 -> x0, other arithmetic: 1.11 us -> none  [per_device(): return ((2.0 * rates / width)[:, None] * moved, grad_coef)]
where the time goes in v4:
time: 60.6 us; the launch traced here: 60.5 us
  Pallas kernels  55.6 us (92%)
  local copies, waits for them, and re-layouts  3.68 us (6%)
  between operations  0.66 us (1%)
    pallas_call x1, Pallas kernels, per_device(): pl.pallas_call(functools.partial(body, Z, C), out_shape=(jax.ShapeDtypeSt...  55.6 us
    unnamed x6, local copies, waits for them, and re-layouts  3.68 us

profile of v4, /device:TPU:0, one launch (start us, length us, event | category | flops | bytes accessed | tf_op | source)
XLA Modules:
  0.0 60.5 jit_solution(15569386361967742)
XLA Ops:
  0.6 0.0 copy-start.1
  0.6 0.7 %copy-done.1 = bf16[512]{0:T(512)(128)(2,1)S(1)} copy-done((bf16[512]{0:T(512)(128)(2,1)S(1)}, bf16[512]{0:T(512)(128)(2,1)}, u32[]{:S(2)}) %copy-start.1) | copy-done | bytes 1048
  1.3 0.6 reshape.27
  1.9 55.6 %shard_map.86 = (f32[512,512]{1,0:T(8,128)}, f32[512,128]{1,0:T(8,128)}) custom-call(bf16[4,256,512]{2,1,0:T(8,128)(2,1)} %bitcast.6, f32[4,256,128]{2,1,0:T(8,128)} %bitcast.7, f32[4,256,128]{2,1,0:T(8,128)} %bitcast.8, f32[1,128]{1,0:T(1,128)} %bitcast.9, f32[1,512]{1,0:T(1,128)} %bitcast.5, bf16[512,512]{1,0:T(8,128)(2,1)} %cen_in.1, bf16[512,128]{1,0:T(8,128)(2,1)} %coef_in.1), custom_call_target="tpu_custom_call" | custom-call | flops 5905580032 | bytes 4194304 | tf_op jit(solution)/shard_map/pallas_call | solution.py:363
  57.5 0.0 copy-start
  57.5 2.3 %copy.11 = f32[512,512]{1,0:T(8,128)} copy(f32[512,512]{1,0:T(8,128)} %get-tuple-element.4) | data formatting | bytes 2097152
  59.8 0.0 copy-done
  59.8 0.7 %copy.12 = f32[512,128]{1,0:T(8,128)} copy(f32[512,128]{1,0:T(8,128)S(1)} %copy-done) | data formatting | bytes 524288
Async XLA Ops:
  0.6 0.7 %copy-start.1 = (bf16[512]{0:T(512)(128)(2,1)S(1)}, bf16[512]{0:T(512)(128)(2,1)}, u32[]{:S(2)}) copy-start(bf16[512]{0:T(512)(128)(2,1)} %param.13) | copy-start | bytes 3076
  57.5 2.3 %copy-start = (f32[512,128]{1,0:T(8,128)S(1)}, f32[512,128]{1,0:T(8,128)}, u32[]{:S(2)}) copy-start(f32[512,128]{1,0:T(8,128)} %get-tuple-element.5) | copy-start | bytes 786436

commit v5 on v4

--- a/solution.py
+++ b/solution.py
@@ -216,10 +216,29 @@
             for k in range(1, X):
                 xcopy(b, k, s).start()
 
+    def own_lanes(b):
+        for s in range(SUBS):
+            ccopy(b, x, s, coming=True).wait_recv()
+
     def work(b):
-        for s in range(SUBS):
-            ccopy(b, x, s, coming=True).wait_recv()
+        own_lanes(b)
         forward_own(b)
+
+    def forward_all(b):
+        own_lanes(b)
+        for co in (other, core):
+            t = lane(x, co)
+            rows_t = pts[b, t].T
+            psq = square_sum(rows_t)
+            k = kernel_of(rows_t, psq, x)
+            kt[b, :, cols_of(t)] = k
+            total = jnp.dot(coeft[x], k, preferred_element_type=f32)
+            for i in range(1, X):
+                k = kernel_of(rows_t, psq, off[i])
+                total = total + jnp.dot(coeft[off[i]], k, preferred_element_type=f32)
+            pred[b, co] = total
+            if co is other:
+                pccopy(b).start()
 
     def finish(b):
         pccopy(b).wait_recv()
@@ -255,19 +274,17 @@
         prepare(back[k])
 
     def middle(d, carry):
-        @pl.when((d >= 1) & (d < Z - 1))
-        def _():
-            blocks(d, send_x)
-
-        @pl.when(d == Z - 1)
-        def _():
-            arrivals(d)
-            blocks(d, send_x)
-            blocks(d, work)
+        blocks(d, send_x)
         blocks(d, forward_rest, 0)
         blocks(d - 1, finish, 0)
         return carry
-    lax.fori_loop(0, Z + 1, middle, 0)
+    lax.fori_loop(0, Z - 1, middle, 0)
+    blocks(Z - 2, finish, 0)
+    arrivals(Z - 1)
+    blocks(Z - 1, send_x)
+    blocks(Z - 1, forward_all)
+    blocks(Z - 1, finish)
+    blocks(1, rest)
 
     total = psum[z]
     for k in range(1, Z):
@@ -303,19 +320,23 @@
 
     spread_cot(z)
 
+    blocks(2, rest)
+    blocks(1, cot_arrive)
+    cot_cross(z)
+    cot_work(z)
+
     def late(d, carry):
+        blocks(d - 1, cot_arrive)
         blocks(d, rest)
-        blocks(d, cot_arrive)
         return carry
-    lax.fori_loop(1, Z, late, 0)
-
-    cot_cross(z)
+    lax.fori_loop(3, Z + 1, late, 0)
+    blocks(1, cot_cross)
 
     def last(d, carry):
         blocks(d + 1, cot_cross)
-        blocks(d, cot_work, 0)
+        blocks(d, cot_work)
         return carry
-    lax.fori_loop(0, Z, last, 0)
+    lax.fori_loop(1, Z, last, 0)
 
     row_totals = jnp.sum(tot[...], axis=1, keepdims=True)
     scale = (-2.0 / LOG2E) * nrate[x]
@@ -362,8 +383,7 @@
     flops = 2 * Z * n_points * n_cen * (2 * width + 3 * n_out)
     return tuple(pl.pallas_call(
         functools.partial(body, Z, C),
-        out_shape=(jax.ShapeDtypeStruct((n_cen, width), f32),
-                   jax.ShapeDtypeStruct((n_cen, n_out), f32)),
+        out_shape=(pltpu.VMEM((n_cen, width), f32), pltpu.VMEM((n_cen, n_out), f32)),
         in_specs=[in_hbm] * 7,
         out_specs=(vm, vm),
         scratch_shapes=[

time: 60.6 us -> 59.6 us (0.983)
  local copies, waits for them, and re-layouts: 3.68 us -> 2.35 us
    unnamed x6 -> x4, local copies, waits for them, and re-layouts: 3.68 us -> 2.35 us
where the time goes in v5:
time: 59.6 us; the launch traced here: 59.4 us
  Pallas kernels  55.8 us (94%)
  local copies, waits for them, and re-layouts  2.35 us (4%)
  between operations  0.65 us (1%)
    pallas_call x1, Pallas kernels, per_device(): pl.pallas_call(functools.partial(body, Z, C), out_shape=(pltpu.VMEM((n_ce...  55.8 us
    unnamed x4, local copies, waits for them, and re-layouts  2.35 us

profile of v5, /device:TPU:0, one launch (start us, length us, event | category | flops | bytes accessed | tf_op | source)
XLA Modules:
  0.0 59.4 jit_solution(1990592865813021432)
XLA Ops:
  0.6 0.0 copy-start
  0.6 0.7 %copy-done = bf16[512]{0:T(512)(128)(2,1)S(1)} copy-done((bf16[512]{0:T(512)(128)(2,1)S(1)}, bf16[512]{0:T(512)(128)(2,1)}, u32[]{:S(2)}) %copy-start) | copy-done | bytes 1048
  1.3 0.6 reshape.27
  1.9 55.8 %shard_map.86 = (f32[512,512]{1,0:T(8,128)S(1)}, f32[512,128]{1,0:T(8,128)S(1)}) custom-call(bf16[4,256,512]{2,1,0:T(8,128)(2,1)} %bitcast.6, f32[4,256,128]{2,1,0:T(8,128)} %bitcast.7, f32[4,256,128]{2,1,0:T(8,128)} %bitcast.8, f32[1,128]{1,0:T(1,128)} %bitcast.9, f32[1,512]{1,0:T(1,128)} %bitcast.5, bf16[512,512]{1,0:T(8,128)(2,1)} %cen_in.1, ...), custom_call_target="tpu_custom_call" | custom-call | flops 5905580032 | bytes 4194304 | tf_op jit(solution)/shard_map/pallas_call | solution.py:384
  57.7 1.0 %copy.11 = f32[512,512]{1,0:T(8,128)} copy(f32[512,512]{1,0:T(8,128)S(1)} %get-tuple-element.2) | data formatting | bytes 2097152
  58.7 0.7 %copy.12 = f32[512,128]{1,0:T(8,128)} copy(f32[512,128]{1,0:T(8,128)S(1)} %get-tuple-element.3) | data formatting | bytes 524288
Async XLA Ops:
  0.6 0.7 %copy-start = (bf16[512]{0:T(512)(128)(2,1)S(1)}, bf16[512]{0:T(512)(128)(2,1)}, u32[]{:S(2)}) copy-start(bf16[512]{0:T(512)(128)(2,1)} %param.13) | copy-start | bytes 3076

commit v6 on v5

--- a/solution.py
+++ b/solution.py
@@ -271,10 +271,15 @@
     for k in range(1, X):
         for copy in ecopies(k, coming=True):
             copy.wait_recv()
+
+    def send_early(d, carry):
+        blocks(d, send_x)
+        return carry
+    lax.fori_loop(1, Z - 1, send_early, 0)
+    for k in range(1, X):
         prepare(back[k])
 
     def middle(d, carry):
-        blocks(d, send_x)
         blocks(d, forward_rest, 0)
         blocks(d - 1, finish, 0)
         return carry
@@ -284,7 +289,6 @@
     blocks(Z - 1, send_x)
     blocks(Z - 1, forward_all)
     blocks(Z - 1, finish)
-    blocks(1, rest)
 
     total = psum[z]
     for k in range(1, Z):
@@ -320,20 +324,20 @@
 
     spread_cot(z)
 
-    blocks(2, rest)
+    blocks(1, rest)
     blocks(1, cot_arrive)
+    blocks(2, cot_arrive)
     cot_cross(z)
     cot_work(z)
 
     def late(d, carry):
-        blocks(d - 1, cot_arrive)
-        blocks(d, rest)
-        return carry
-    lax.fori_loop(3, Z + 1, late, 0)
-    blocks(1, cot_cross)
+        blocks(d, cot_arrive)
+        return carry
+    lax.fori_loop(3, Z, late, 0)
 
     def last(d, carry):
-        blocks(d + 1, cot_cross)
+        blocks(d, cot_cross)
+        blocks(d + 1, rest)
         blocks(d, cot_work)
         return carry
     lax.fori_loop(1, Z, last, 0)

time: 59.6 us -> 60.8 us (1.020); the launches traced: 59.4 us -> 59.9 us
  no operation moved by 1% of the time
where the time goes in v6:
time: 60.8 us; the launch traced here: 59.9 us
  Pallas kernels  56.3 us (93%)
  local copies, waits for them, and re-layouts  2.35 us (4%)
  between operations  0.65 us (1%)
    pallas_call x1, Pallas kernels, per_device(): pl.pallas_call(functools.partial(body, Z, C), out_shape=(pltpu.VMEM((n_ce...  56.3 us
    unnamed x4, local copies, waits for them, and re-layouts  2.35 us

profile of v6, /device:TPU:0, one launch (start us, length us, event | category | flops | bytes accessed | tf_op | source)
XLA Modules:
  0.0 59.9 jit_solution(2112669045917414117)
XLA Ops:
  0.6 0.0 copy-start
  0.6 0.7 %copy-done = bf16[512]{0:T(512)(128)(2,1)S(1)} copy-done((bf16[512]{0:T(512)(128)(2,1)S(1)}, bf16[512]{0:T(512)(128)(2,1)}, u32[]{:S(2)}) %copy-start) | copy-done | bytes 1048
  1.3 0.6 reshape.27
  1.9 56.3 %shard_map.86 = (f32[512,512]{1,0:T(8,128)S(1)}, f32[512,128]{1,0:T(8,128)S(1)}) custom-call(bf16[4,256,512]{2,1,0:T(8,128)(2,1)} %bitcast.6, f32[4,256,128]{2,1,0:T(8,128)} %bitcast.7, f32[4,256,128]{2,1,0:T(8,128)} %bitcast.8, f32[1,128]{1,0:T(1,128)} %bitcast.9, f32[1,512]{1,0:T(1,128)} %bitcast.5, bf16[512,512]{1,0:T(8,128)(2,1)} %cen_in.1, ...), custom_call_target="tpu_custom_call" | custom-call | flops 5905580032 | bytes 4194304 | tf_op jit(solution)/shard_map/pallas_call | solution.py:388
  58.2 1.0 %copy.11 = f32[512,512]{1,0:T(8,128)} copy(f32[512,512]{1,0:T(8,128)S(1)} %get-tuple-element.2) | data formatting | bytes 2097152
  59.2 0.7 %copy.12 = f32[512,128]{1,0:T(8,128)} copy(f32[512,128]{1,0:T(8,128)S(1)} %get-tuple-element.3) | data formatting | bytes 524288
Async XLA Ops:
  0.6 0.7 %copy-start = (bf16[512]{0:T(512)(128)(2,1)S(1)}, bf16[512]{0:T(512)(128)(2,1)}, u32[]{:S(2)}) copy-start(bf16[512]{0:T(512)(128)(2,1)} %param.13) | copy-start | bytes 3076

commit v7 on v5

--- a/solution.py
+++ b/solution.py
@@ -136,10 +136,17 @@
     tot[...] = jnp.zeros_like(tot)
 
     def wide(col):
-        return jnp.concatenate([col] * (q // 128), axis=1)
-
-    def cols_of(t):
-        return pl.ds(pl.multiple_of(t * q, q), q)
+        return jnp.concatenate([col] * (CORES * q // 128), axis=1)
+
+    def cols_of(xi):
+        return pl.ds(pl.multiple_of(xi * CORES * q, CORES * q), CORES * q)
+
+    def rows_of(b, xi):
+        return pts[b, pl.ds(xi * CORES, CORES)].reshape(CORES * q, width).T
+
+    def put_pred(b, total):
+        for co in range(CORES):
+            pred[b, co] = total[:, co * q:(co + 1) * q]
 
     def square_sum(rows_t):
         r32 = rows_t.astype(f32)
@@ -151,33 +158,27 @@
         return jnp.exp2(wide(nrate[xi]) * dist).astype(bf16)
 
     def forward_own(b):
-        for co in (other, core):
-            t = lane(x, co)
-            rows_t = pts[b, t].T
-            psq = square_sum(rows_t)
-            ptst[b, co] = rows_t
-            psqs[b, co] = psq
-            k = kernel_of(rows_t, psq, x)
-            kt[b, :, cols_of(t)] = k
-            pred[b, co] = jnp.dot(coeft[x], k, preferred_element_type=f32)
+        rows_t = rows_of(b, x)
+        psq = square_sum(rows_t)
+        ptst[b] = rows_t
+        psqs[b] = psq
+        k = kernel_of(rows_t, psq, x)
+        kt[b, :, cols_of(x)] = k
+        put_pred(b, jnp.dot(coeft[x], k, preferred_element_type=f32))
 
     def forward_rest(b):
-        for co in (other, core):
-            rows_t, psq = ptst[b, co], psqs[b, co]
-            total = pred[b, co]
-            for i in range(1, X):
-                k = kernel_of(rows_t, psq, off[i])
-                total = total + jnp.dot(coeft[off[i]], k, preferred_element_type=f32)
-            pred[b, co] = total
-            if co is other:
-                pccopy(b).start()
+        rows_t, psq = ptst[b], psqs[b]
+        total = jnp.concatenate([pred[b, co] for co in range(CORES)], axis=1)
+        for i in range(1, X):
+            k = kernel_of(rows_t, psq, off[i])
+            total = total + jnp.dot(coeft[off[i]], k, preferred_element_type=f32)
+        put_pred(b, total)
+        pccopy(b).start()
 
     def kernel_rest(b):
         for i in range(1, X):
-            for co in (core, other):
-                t = lane(back[i], co)
-                rows_t = pts[b, t].T
-                kt[b, :, cols_of(t)] = kernel_of(rows_t, square_sum(rows_t), x)
+            rows_t = rows_of(b, back[i])
+            kt[b, :, cols_of(back[i])] = kernel_of(rows_t, square_sum(rows_t), x)
 
     def backward(b):
         for t in range(C):
@@ -226,19 +227,16 @@
 
     def forward_all(b):
         own_lanes(b)
-        for co in (other, core):
-            t = lane(x, co)
-            rows_t = pts[b, t].T
-            psq = square_sum(rows_t)
-            k = kernel_of(rows_t, psq, x)
-            kt[b, :, cols_of(t)] = k
-            total = jnp.dot(coeft[x], k, preferred_element_type=f32)
-            for i in range(1, X):
-                k = kernel_of(rows_t, psq, off[i])
-                total = total + jnp.dot(coeft[off[i]], k, preferred_element_type=f32)
-            pred[b, co] = total
-            if co is other:
-                pccopy(b).start()
+        rows_t = rows_of(b, x)
+        psq = square_sum(rows_t)
+        k = kernel_of(rows_t, psq, x)
+        kt[b, :, cols_of(x)] = k
+        total = jnp.dot(coeft[x], k, preferred_element_type=f32)
+        for i in range(1, X):
+            k = kernel_of(rows_t, psq, off[i])
+            total = total + jnp.dot(coeft[off[i]], k, preferred_element_type=f32)
+        put_pred(b, total)
+        pccopy(b).start()
 
     def finish(b):
         pccopy(b).wait_recv()
@@ -284,7 +282,6 @@
     blocks(Z - 1, send_x)
     blocks(Z - 1, forward_all)
     blocks(Z - 1, finish)
-    blocks(1, rest)
 
     total = psum[z]
     for k in range(1, Z):
@@ -320,8 +317,9 @@
 
     spread_cot(z)
 
+    blocks(1, rest)
+    blocks(1, cot_arrive)
     blocks(2, rest)
-    blocks(1, cot_arrive)
     cot_cross(z)
     cot_work(z)
 
@@ -388,8 +386,8 @@
         out_specs=(vm, vm),
         scratch_shapes=[
             pltpu.VMEM((Z, C, q, width), bf16),
-            pltpu.VMEM((Z, CORES, width, q), bf16),
-            pltpu.VMEM((Z, CORES, 1, q), f32),
+            pltpu.VMEM((Z, width, CORES * q), bf16),
+            pltpu.VMEM((Z, 1, CORES * q), f32),
             pltpu.VMEM((Z, n_cen, C * q), bf16),
             pltpu.VMEM((Z, CORES, n_out, q), f32),
             pltpu.VMEM((Z, n_out, q), f32),

time: 59.6 us -> 58.7 us (0.985); the launches traced: 59.4 us -> 57.6 us
  Pallas kernels: 55.8 us -> 54 us
    pallas_call x1, Pallas kernels: 55.8 us -> 54 us  [per_device(): pl.pallas_call(functools.partial(body, Z, C), out_shape=(pltpu.VMEM((n_ce...]
where the time goes in v7:
time: 58.7 us; the launch traced here: 57.6 us
  Pallas kernels  54 us (92%)
  local copies, waits for them, and re-layouts  2.35 us (4%)
  between operations  0.65 us (1%)
    pallas_call x1, Pallas kernels, per_device(): pl.pallas_call(functools.partial(body, Z, C), out_shape=(pltpu.VMEM((n_ce...  54 us
    unnamed x4, local copies, waits for them, and re-layouts  2.35 us

profile of v7, /device:TPU:0, one launch (start us, length us, event | category | flops | bytes accessed | tf_op | source)
XLA Modules:
  0.0 57.6 jit_solution(8147013773070455399)
XLA Ops:
  0.6 0.0 copy-start
  0.6 0.7 %copy-done = bf16[512]{0:T(512)(128)(2,1)S(1)} copy-done((bf16[512]{0:T(512)(128)(2,1)S(1)}, bf16[512]{0:T(512)(128)(2,1)}, u32[]{:S(2)}) %copy-start) | copy-done | bytes 1048
  1.3 0.6 %reshape.27 = f32[512]{0:T(512)} convert(bf16[512]{0:T(512)(128)(2,1)S(1)} %copy-done) | non-fusion elementwise | flops 512 | bytes 3072 | tf_op jit(solution)/shard_map/reshape | solution.py:426
  1.9 54.0 %shard_map.86 = (f32[512,512]{1,0:T(8,128)S(1)}, f32[512,128]{1,0:T(8,128)S(1)}) custom-call(bf16[4,256,512]{2,1,0:T(8,128)(2,1)} %bitcast.6, f32[4,256,128]{2,1,0:T(8,128)} %bitcast.7, f32[4,256,128]{2,1,0:T(8,128)} %bitcast.8, f32[1,128]{1,0:T(1,128)} %bitcast.9, f32[1,512]{1,0:T(1,128)} %bitcast.5, bf16[512,512]{1,0:T(8,128)(2,1)} %cen_in.1, ...), custom_call_target="tpu_custom_call" | custom-call | flops 5905580032 | bytes 4194304 | tf_op jit(solution)/shard_map/pallas_call | solution.py:382
  55.9 1.0 %copy.11 = f32[512,512]{1,0:T(8,128)} copy(f32[512,512]{1,0:T(8,128)S(1)} %get-tuple-element.2) | data formatting | bytes 2097152
  56.9 0.7 %copy.12 = f32[512,128]{1,0:T(8,128)} copy(f32[512,128]{1,0:T(8,128)S(1)} %get-tuple-element.3) | data formatting | bytes 524288
Async XLA Ops:
  0.6 0.7 %copy-start = (bf16[512]{0:T(512)(128)(2,1)S(1)}, bf16[512]{0:T(512)(128)(2,1)}, u32[]{:S(2)}) copy-start(bf16[512]{0:T(512)(128)(2,1)} %param.13) | copy-start | bytes 3076

commit v8 on v7

--- a/solution.py
+++ b/solution.py
@@ -57,7 +57,7 @@
         at = back[k] if coming else x
         return [remote(src, dst.at[at], es.at[k, i], er.at[k, i], centers=lane(off[k], core))
                 for i, (src, dst) in enumerate(
-                    ((cen_in, cen), (coef_in, coef), (rates_in, rates)))]
+                    ((cen_in, cen), (coef_in, coef), (rates.at[x], rates)))]
 
     def pccopy(b):
         return remote(pred.at[b, other], pc.at[b], pcs.at[b], pcr.at[b], centers=mate)
@@ -100,8 +100,9 @@
     own_points.start()
     own_saved.start()
     own_target.start()
+    rates[x] = rates_in[...].astype(f32).reshape(1, rates.shape[2])
     small = [pltpu.make_async_copy(a, b, ls.at[3 + i]) for i, (a, b) in enumerate(
-        ((cen_in, cen.at[x]), (coef_in, coef.at[x]), (rates_in, rates.at[x]), (delta_in, delta)))]
+        ((cen_in, cen.at[x]), (coef_in, coef.at[x]), (delta_in, delta)))]
     for copy in small:
         copy.start()
     pl.semaphore_wait(barrier, Z - 1 + X - 1 + 1)
@@ -382,7 +383,7 @@
     return tuple(pl.pallas_call(
         functools.partial(body, Z, C),
         out_shape=(pltpu.VMEM((n_cen, width), f32), pltpu.VMEM((n_cen, n_out), f32)),
-        in_specs=[in_hbm] * 7,
+        in_specs=[in_hbm] * 4 + [vm] + [in_hbm] * 2,
         out_specs=(vm, vm),
         scratch_shapes=[
             pltpu.VMEM((Z, C, q, width), bf16),
@@ -423,7 +424,7 @@
             flops=flops, bytes_accessed=4 << 20, transcendentals=Z * n_points * n_cen),
     )(train_points.reshape(C, q, width), saved_preds.reshape(C, q, n_out),
       targets.reshape(C, q, n_out), huber_delta.reshape(1, n_out),
-      spread.astype(f32).reshape(1, n_cen), center_pos, coefficients))
+      spread, center_pos, coefficients))
 
 
 def solution(mesh):

time: 58.7 us -> 58.1 us (0.990)
  Pallas kernels: 54 us -> 54.7 us
  local copies, waits for them, and re-layouts: 2.35 us -> 1.67 us
    pallas_call x1, Pallas kernels: 54 us -> 54.7 us  [per_device(): pl.pallas_call(functools.partial(body, Z, C), out_shape=(pltpu.VMEM((n_ce...]
    unnamed x4 -> x2, local copies, waits for them, and re-layouts: 2.35 us -> 1.67 us
where the time goes in v8:
time: 58.1 us; the launch traced here: 57 us
  Pallas kernels  54.7 us (94%)
  local copies, waits for them, and re-layouts  1.67 us (3%)
  between operations  0.64 us (1%)
    pallas_call x1, Pallas kernels, per_device(): pl.pallas_call(functools.partial(body, Z, C), out_shape=(pltpu.VMEM((n_ce...  54.7 us
    unnamed x2, local copies, waits for them, and re-layouts  1.67 us

profile of v8, /device:TPU:0, one launch (start us, length us, event | category | flops | bytes accessed | tf_op | source)
XLA Modules:
  0.0 57.0 jit_solution(13825378374928784643)
XLA Ops:
  0.6 54.7 %shard_map.86 = (f32[512,512]{1,0:T(8,128)S(1)}, f32[512,128]{1,0:T(8,128)S(1)}) custom-call(bf16[4,256,512]{2,1,0:T(8,128)(2,1)} %bitcast.4, f32[4,256,128]{2,1,0:T(8,128)} %bitcast.5, f32[4,256,128]{2,1,0:T(8,128)} %bitcast.6, f32[1,128]{1,0:T(1,128)} %bitcast.7, bf16[512]{0:T(512)(128)(2,1)} %rates_in.1, bf16[512,512]{1,0:T(8,128)(2,1)} %cen_in.1, ...), custom_call_target="tpu_custom_call" | custom-call | flops 5905580032 | bytes 4194304 | tf_op jit(solution)/shard_map/pallas_call | solution.py:383
  55.3 1.0 %copy.11 = f32[512,512]{1,0:T(8,128)} copy(f32[512,512]{1,0:T(8,128)S(1)} %get-tuple-element.2) | data formatting | bytes 2097152
  56.3 0.7 %copy.12 = f32[512,128]{1,0:T(8,128)} copy(f32[512,128]{1,0:T(8,128)S(1)} %get-tuple-element.3) | data formatting | bytes 524288
